TPU v7x, 128 devices: a whole 4x4x4 slice. The times are simulated.
128 devices in a mesh: leaf: 16 (over x_lo, z, core), sub: 8 (over x_hi, y).
Axes of the slice: x: 4 (x_hi: 2, x_lo: 2; x = x_hi * 2 + x_lo), y: 4, z: 4, core: 2. Of those that a mesh axis runs over, the one named last changes fastest.
Arguments:
- density: bfloat16 [32, 2097152], P(None, ('leaf', 'sub')), may hold values from -6 to 6
- geometry: float32 [8192, 6, 256], P(('leaf', 'sub')), may hold values from -134 to 134
- near_list: int32 [8192, 9], P(('leaf', 'sub')), may hold values from 0 to 8191, as said below
- near_count: int32 [8192], P(('leaf', 'sub')), may hold values from 1 to 9, as said below
- far_list: int32 [8192, 16], P(('leaf', 'sub')), may hold values from 0 to 8191, as said below
- bases: bfloat16 [8192, 64, 256], P(('leaf', 'sub')), may hold values from -0.375 to 0.375
- proxies: float32 [8192, 3, 64], P(('leaf', 'sub')), may hold values from -134 to 134
- leaf_transfer: bfloat16 [8192, 64, 64], P(('leaf', 'sub')), may hold values from -0.25 to 0.25
- parent_transfer: bfloat16 [1024, 64, 64], P(('leaf', 'sub')), may hold values from -0.75 to 0.75
- top_proxies: float32 [16, 3, 64], replicated, may hold values from -4 to 4
- top_far: int32 [16, 8], replicated, may hold values from 0 to 15, as said below
Outputs:
- product: float32 [32, 2097152], P(None, ('leaf', 'sub'))
Inputs may be any that keep to these rules, and one draw needn't show every extreme that they name: `near_list`: slot 0 of row t is t itself; the other slots hold, in an order drawn for each leaf, the eight leaves t + a * 31 + b modulo 8192 with a and b each -1, 0 or 1, not both 0. `near_count`: the live slots on the leaves of one device number at most 416 together, and exactly 416 on one device. `far_list`: row t holds sixteen distinct leaves, in an order drawn for each leaf, chosen for each leaf from the twenty-two leaves t + a * 31 + b modulo 8192 with a from -2 to 2, b from -3 to 3, and either the larger of |a| and |b| equal to 2, or |a| at most 1 and |b| equal to 3. `top_far`: distinct nodes, none equal to the node or to its two cyclic neighbours.
All inputs are finite; a program needn't handle non-finite values.
Results may differ from a plain program's by a relative error of at most 0.007.
Values may be sent and summed in bfloat16 or wider, within the bound.
No kernel may reach another device: no remote copies, remote signals or barrier semaphores. Data moves between devices by JAX's collectives and lax.ppermute only.
A program may use at most 64 MiB of HBM per device.

v0:
```python
import math

import jax
import jax.numpy as jnp
from jax import lax
from jax.experimental import pallas as pl
from jax.experimental.pallas import tpu as pltpu
from jax.sharding import PartitionSpec as P

SOFTEN = 0.01
FOUR_PI = 4.0 * math.pi
AXES = ("leaf", "sub")
LANES = 128
CHUNK = 16
SMEM = pl.BlockSpec(memory_space=pltpu.SMEM)
VMEM = pl.BlockSpec(memory_space=pltpu.VMEM)
PARAMS = pltpu.CompilerParams(vmem_limit_bytes=48 * 1024 * 1024)


def product(left, right, left_dim=1, right_dim=0):
    return lax.dot_general(
        left, right, (((left_dim,), (right_dim,)), ((), ())), preferred_element_type=jnp.float32
    )


def local(leaf, first, total):
    moved = leaf - first + (total + total // 2)
    if total & (total - 1) == 0:
        return (moved & (total - 1)) - total // 2
    return lax.rem(moved, total) - total // 2


def lift_kernel(density, bases, leaf_transfer, parent_transfer, coefficients, partial):
    fan, _, width = bases.shape

    @pl.when(pl.program_id(0) == 0)
    def _():
        partial[...] = jnp.zeros_like(partial)

    values = [
        product(density[:, c * width : (c + 1) * width], bases[c], 1, 1).astype(jnp.bfloat16)
        for c in range(fan)
    ]
    lifted = sum(product(value, leaf_transfer[c]) for c, value in enumerate(values))
    for c in range(0, fan, 2):
        coefficients[c // 2] = jnp.concatenate(values[c : c + 2], axis=1)
    partial[...] += product(lifted.astype(jnp.bfloat16), parent_transfer[0])


def lift(density, bases, leaf_transfer, parent_transfer):
    leaves, rank, width = bases.shape
    sides = density.shape[0]
    parents = parent_transfer.shape[0]
    fan = leaves // parents
    return pl.pallas_call(
        lift_kernel,
        grid=(parents,),
        out_shape=(
            jax.ShapeDtypeStruct((leaves // 2, sides, 2 * rank), jnp.bfloat16),
            jax.ShapeDtypeStruct((sides, rank), jnp.float32),
        ),
        in_specs=[
            pl.BlockSpec((sides, fan * width), lambda p: (0, p)),
            pl.BlockSpec((fan, rank, width), lambda p: (p, 0, 0)),
            pl.BlockSpec((fan, rank, rank), lambda p: (p, 0, 0)),
            pl.BlockSpec((1, rank, rank), lambda p: (p, 0, 0)),
        ],
        out_specs=(
            pl.BlockSpec((fan // 2, sides, 2 * rank), lambda p: (p, 0, 0)),
            pl.BlockSpec((sides, rank), lambda p: (0, 0)),
        ),
        compiler_params=pltpu.CompilerParams(vmem_limit_bytes=60 * 1024 * 1024),
    )(density, bases, leaf_transfer, parent_transfer)


def split(value):
    high = value.astype(jnp.bfloat16).astype(jnp.float32)
    left = value - high
    middle = left.astype(jnp.bfloat16).astype(jnp.float32)
    return high, middle, left - middle


def near_kernel(
    place, near_list, other_list,
    geo_own, geo_low, geo_high, geo_other, geo_side,
    den_own, den_low, den_high, den_other, den_side,
    near, near_other, task_target, task_source, source, target, density, lhs, column,
    flux_one, flux_two, block_one, block_two, sums,
):
    leaves = geo_own.shape[1]
    width = geo_own.shape[2]
    reach = geo_low.shape[1]
    half = leaves // 2
    region = leaves + reach
    everything = 2 * region
    slots = near_list.shape[0] - 1
    side = place[0]

    def put(ref, row, value):
        for b in range(0, width, LANES):
            ref[b // LANES, pl.ds(row, 8, stride=8), :] = value[:, b : b + LANES]

    def get(ref, row, count):
        return jnp.concatenate(
            [ref[b, pl.ds(row, count), :] for b in range(width // LANES)], axis=1
        )

    def append(lists, base, shift):
        def leaf(i, position):
            t = side * half + i
            live = lists[slots, t]
            for k in range((slots + 1) // 2):
                task_target[(position >> 1) + k] = i + shift
            for k in range(slots):
                task_source[position] = lists[k, t] + base
                position = position + jnp.where(k < live, 1, 0)
            task_source[position] = everything
            return ((position + 1) >> 1) << 1

        return leaf

    for i in range(2):
        task_target[i] = leaves
        task_source[2 * i] = everything
        task_source[2 * i + 1] = everything
    ended = lax.fori_loop(0, half, append(near_list, 0, 0), 4)
    ended = lax.fori_loop(
        0, half, append(other_list, region, half), ended
    )
    pairs = (ended >> 1) - 2
    for i in range(4):
        task_target[pairs + 2 + i] = leaves
        task_source[ended + 2 * i] = everything
        task_source[ended + 2 * i + 1] = everything

    def table(center, base, geo, den):
        for g in range(0, geo.shape[1], 8):
            position = [geo[c, g : g + 8, :width] for c in range(3)]
            normal = [geo[3 + c, g : g + 8, :width] * (1.0 / FOUR_PI) for c in range(3)]
            moved = [value - middle for value, middle in zip(position, center)]
            shift = normal[0] * moved[0] + normal[1] * moved[1] + normal[2] * moved[2]
            row = (base + g) * 8
            for c in range(3):
                put(source, row + c, normal[c])
                put(source, row + 4 + c, position[c])
            put(source, row + 3, shift)
            put(source, row + 7, jnp.zeros_like(shift))
        for l in range(geo.shape[1]):
            density[base + l] = den[:, l * width : (l + 1) * width]

    def aims(center, base, geo):
        def group(i, _):
            place_in = pl.multiple_of(side * half + i * 8, 8)
            row = (base + i * 8) * 8
            one = jnp.ones((8, width), jnp.float32)
            for c in range(3):
                position = geo[c, pl.ds(place_in, 8), :]
                put(target, row + c, position - center[c])
                put(target, row + 4 + c, position)
            put(target, row + 3, -one)
            put(target, row + 7, 0.0 * one)
            return 0

        lax.fori_loop(0, half // 8, group, 0, unroll=True)

    center = [jnp.mean(geo_own[c], keepdims=True) for c in range(3)]
    table(center, 0, geo_own, den_own)

    @pl.when(side == 0)
    def _():
        table(center, leaves, geo_low, den_low)

    @pl.when(side != 0)
    def _():
        table(center, leaves, geo_high, den_high)

    aims(center, 0, geo_own)
    center = [jnp.mean(geo_other[c], keepdims=True) for c in range(3)]
    table(center, region, geo_other, den_other)
    table(center, region + leaves, geo_side, den_side)
    aims(center, half, geo_other)
    density[everything] = jnp.zeros(density.shape[1:], density.dtype)
    for b in range(width // LANES):
        source[b, everything * 8 :, :] = jnp.zeros((8, LANES), jnp.float32)

    rows = lax.broadcasted_iota(jnp.int32, (8, width), 0)
    with_shift = (rows < 4).astype(jnp.float32)
    without = (rows < 3).astype(jnp.float32)

    def prepare(t, _):
        raw = get(target, pl.multiple_of(t * 8, 8), 8)
        high, middle, low = split(raw)
        led = high * with_shift
        second = middle * without
        stacked = jnp.concatenate([led, second, low * without, led, second, led, raw], axis=0)
        turned = stacked.T
        lhs[t] = turned[:, :48].astype(jnp.bfloat16)
        column[t] = turned[:, 48:]
        sums[t] = jnp.zeros(sums.shape[1:], sums.dtype)
        return 0

    lax.fori_loop(0, leaves, prepare, 0, unroll=8)
    sums[leaves] = jnp.zeros(sums.shape[1:], sums.dtype)
    for ref in (flux_one, flux_two, block_one, block_two):
        ref[...] = jnp.zeros_like(ref)

    def weights(s):
        high, middle, low = split(get(source, pl.multiple_of(s * 8, 8), 8))
        return jnp.concatenate([high, high, high, middle, middle, low], axis=0).astype(jnp.bfloat16)

    def multiply(j, block):
        both = jnp.concatenate([density[task_source[2 * j + i]] for i in range(2)], axis=1)
        sums[task_target[j]] += product(both, block[...], 1, 1)

    def evaluate(j, flux, block):
        t = jnp.minimum(task_target[j], leaves - 1)
        pair = [task_source[2 * j + i] for i in range(2)]
        places = [
            jnp.concatenate([get(source, s * 8 + 4 + a, 1) for s in pair], axis=1)
            for a in range(3)
        ]
        for r in range(0, width, CHUNK):
            lines = column[t, r : r + CHUNK, :]
            spread = [
                jnp.broadcast_to(lines[:, 4 + a : 5 + a], (CHUNK, LANES)) for a in range(3)
            ]
            for b in range(0, 2 * width, LANES):
                gap = [spread[a] - places[a][:, b : b + LANES] for a in range(3)]
                squared = gap[0] * gap[0] + gap[1] * gap[1] + (gap[2] * gap[2] + SOFTEN)
                inverse = lax.rsqrt(squared)
                value = flux[r : r + CHUNK, b : b + LANES] * inverse * (inverse * inverse)
                block[r : r + CHUNK, b : b + LANES] = value.astype(jnp.bfloat16)

    def project(j, flux):
        t = jnp.minimum(task_target[j], leaves - 1)
        pair = [task_source[2 * j + i] for i in range(2)]
        flux[...] = product(lhs[t], jnp.concatenate([weights(s) for s in pair], axis=1))

    def step(i, _):
        j = 2 * i
        multiply(j, block_one)
        evaluate(j + 1, flux_two, block_two)
        project(j + 2, flux_one)
        multiply(j + 1, block_two)
        evaluate(j + 2, flux_one, block_one)
        project(j + 3, flux_two)
        return 0

    lax.fori_loop(0, (pairs + 3) >> 1, step, 0)
    for t in range(half):
        near[t] = sums[t]
        near_other[t] = sums[half + t].astype(near_other.dtype)


def near_field(place, lists, geometries, densities):
    leaves, width = geometries[0].shape[1:]
    everything = 2 * (leaves + geometries[1].shape[1])
    sides = densities[0].shape[0]
    slots = lists[0].shape[0] - 1
    most = leaves * (slots // 2 + 1) + 16
    half = (leaves // 2, sides, width)
    return pl.pallas_call(
        near_kernel,
        out_shape=(
            jax.ShapeDtypeStruct(half, jnp.float32),
            jax.ShapeDtypeStruct(half, jnp.bfloat16),
        ),
        in_specs=[SMEM] * 3 + [VMEM] * 10,
        out_specs=(VMEM, VMEM),
        scratch_shapes=[
            pltpu.SMEM((most,), jnp.int32),
            pltpu.SMEM((2 * most,), jnp.int32),
            pltpu.VMEM((width // LANES, (everything + 1) * 8, LANES), jnp.float32),
            pltpu.VMEM((width // LANES, leaves * 8, LANES), jnp.float32),
            pltpu.VMEM((everything + 1, sides, width), jnp.bfloat16),
            pltpu.VMEM((leaves, width, 48), jnp.bfloat16),
            pltpu.VMEM((leaves, width, 8), jnp.float32),
            pltpu.VMEM((width, 2 * width), jnp.float32),
            pltpu.VMEM((width, 2 * width), jnp.float32),
            pltpu.VMEM((width, 2 * width), jnp.bfloat16),
            pltpu.VMEM((width, 2 * width), jnp.bfloat16),
            pltpu.VMEM((leaves + 1, sides, width), jnp.float32),
        ],
        compiler_params=PARAMS,
        cost_estimate=pl.CostEstimate(
            flops=100 * 10**9 // 2, bytes_accessed=8 * 10**6, transcendentals=3 * 10**7
        ),
    )(place, *lists, *geometries, *densities)


def final_kernel(
    place, far_list, top_far, top_proxies, coupled, coef_own, coef_low, coef_high,
    prox_own, prox_low, prox_high, near, near_back, density, bases, leaf_transfer, parent_transfer,
    out, charges, points, lines, parent_local, far,
):
    leaves, rank, width = bases.shape
    group = place[1]
    half = near.shape[0]
    parents = parent_transfer.shape[0]
    fan = leaves // parents
    sides = density.shape[0]
    left = lax.broadcasted_iota(jnp.int32, (sides, LANES), 1) < rank
    row_left = lax.broadcasted_iota(jnp.int32, (1, LANES), 1) < rank

    def duplicate(value):
        return jnp.concatenate([value, value], axis=1)

    top_local = jnp.zeros((sides, rank), jnp.float32)
    stacked = jnp.concatenate(
        [top_proxies[c, pl.ds(group, 1), :] for c in range(3)]
        + [jnp.zeros((5, rank), jnp.float32)], axis=0,
    )
    turned = duplicate(stacked).T[:rank]
    for k in range(top_far.shape[0]):
        node = top_far[k, group]
        squared = jnp.full((rank, rank), SOFTEN, jnp.float32)
        for c in range(3):
            gap = turned[:, c : c + 1] - top_proxies[c, pl.ds(node, 1), :]
            squared = squared + gap * gap
        coupling = (lax.rsqrt(squared) * (1.0 / FOUR_PI)).astype(jnp.bfloat16)
        top_local = top_local + product(coupled[group ^ node], coupling, 1, 1)
    top_local = top_local.astype(jnp.bfloat16)
    for p in range(parents):
        parent_local[p] = product(top_local, parent_transfer[p], 1, 1).astype(jnp.bfloat16)

    for base, ref, prox in (
        (0, coef_low, prox_low), (leaves, coef_own, prox_own), (2 * leaves, coef_high, prox_high)
    ):
        for i in range(leaves // 2):
            value = ref[i].astype(jnp.float32)
            turned = pltpu.roll(value, rank, 1)
            charges[base + 2 * i] = jnp.where(left, value, turned).astype(jnp.bfloat16)
            charges[base + 2 * i + 1] = jnp.where(left, turned, value).astype(jnp.bfloat16)
        for c in range(3):
            if base == leaves:
                points[c, base : base + leaves, :] = duplicate(prox[c])
                continue
            for b in range(2):
                rows = pl.ds(base + b * (leaves // 2), leaves // 2)
                points[c, rows, :] = duplicate(prox[2 * c + b, :, width : width + rank])
    for g in range(0, leaves, 8):
        for c in range(3):
            lines[pl.ds(g * 8 + c, 8, stride=8), :] = points[c, leaves + g : leaves + g + 8, :]
        for c in range(3, 8):
            lines[pl.ds(g * 8 + c, 8, stride=8), :] = jnp.zeros((8, LANES), jnp.float32)

    def far_leaf(t):
        turned = lines[pl.ds(pl.multiple_of(t * 8, 8), 8), :].T[:rank]
        spread = [jnp.broadcast_to(turned[:, c : c + 1], (rank, LANES)) for c in range(3)]
        blocks = []
        values = []
        for q in range(far_list.shape[0] // 2):
            pair = [far_list[2 * q + i, t] for i in range(2)]
            gap = [
                spread[c]
                - jnp.where(
                    row_left, points[c, pl.ds(pair[0], 1), :], points[c, pl.ds(pair[1], 1), :]
                )
                for c in range(3)
            ]
            squared = gap[0] * gap[0] + gap[1] * gap[1] + (gap[2] * gap[2] + SOFTEN)
            blocks.append((lax.rsqrt(squared) * (1.0 / FOUR_PI)).astype(jnp.bfloat16))
            values.append(jnp.where(left, charges[pair[0]], charges[pair[1]]))
        return product(jnp.concatenate(values, axis=1), jnp.concatenate(blocks, axis=1), 1, 1)

    def far_parent(p):
        for i in range(fan):
            far[i] = far_leaf(fan * p + i)

    def down_parent(p):
        start = pl.multiple_of(p * fan, fan)
        transfer = leaf_transfer[pl.ds(start, fan)].reshape(fan * rank, rank)
        whole = product(parent_local[p], transfer, 1, 1)
        for i in range(fan):
            t = fan * p + i
            leaf_local = (far[i] + whole[:, i * rank : (i + 1) * rank]).astype(jnp.bfloat16)
            span = pl.ds(pl.multiple_of(t * width, width), width)
            row = fan * lax.rem(p, half // fan) + i
            mine = p // (half // fan) == place[0]
            nearby = jnp.where(mine, near[row], near_back[row].astype(jnp.float32))
            result = 0.5 * density[:, span].astype(jnp.float32) + nearby
            out[:, span] = result + product(leaf_local, bases[t])

    def both(p, _):
        down_parent(p)
        far_parent(p + 1)
        return 0

    far_parent(0)
    lax.fori_loop(0, parents - 1, both, 0)
    down_parent(parents - 1)


def finish(place, far_list, top_far, top_proxies, coupled, coefs, proxies, near, near_back, density,
           bases, leaf_transfer, parent_transfer):
    leaves, rank, width = bases.shape
    sides = density.shape[0]
    return pl.pallas_call(
        final_kernel,
        out_shape=jax.ShapeDtypeStruct(density.shape, jnp.float32),
        in_specs=[SMEM] * 3 + [VMEM] * 14,
        out_specs=VMEM,
        scratch_shapes=[
            pltpu.VMEM((3 * leaves, sides, LANES), jnp.bfloat16),
            pltpu.VMEM((3, 3 * leaves, LANES), jnp.float32),
            pltpu.VMEM((leaves * 8, LANES), jnp.float32),
            pltpu.VMEM((parent_transfer.shape[0], sides, rank), jnp.bfloat16),
            pltpu.VMEM((leaves // parent_transfer.shape[0], sides, rank), jnp.float32),
        ],
        compiler_params=PARAMS,
    )(place, far_list, top_far, top_proxies, coupled, *coefs, *proxies, near, near_back, density, bases,
      leaf_transfer, parent_transfer)


def per_device(
    density, geometry, near_list, near_count, far_list, bases, proxies, leaf_transfer,
    parent_transfer, top_proxies, top_far,
):
    leaves, _, width = geometry.shape
    devices = lax.axis_size(AXES)
    total = leaves * devices
    group = lax.axis_index("leaf")
    sub = lax.axis_index("sub")
    subs = lax.axis_size("sub")
    groups = lax.axis_size("leaf")
    side = group % 2
    first = (group * subs + sub) * leaves
    place = jnp.stack([side, group]).astype(jnp.int32)

    def swap(value):
        return lax.ppermute(value, "leaf", [(i, i ^ 1) for i in range(groups)])

    reach = leaves // 2
    forward = [(i, (i + 1) % devices) for i in range(devices)]
    backward = [(b, a) for a, b in forward]
    geometry = jnp.transpose(geometry, (1, 0, 2))
    proxies = jnp.transpose(proxies, (1, 0, 2))
    near_list = jnp.transpose(near_list)
    far_list = jnp.transpose(far_list)
    top_proxies = jnp.transpose(top_proxies, (1, 0, 2))
    top_far = jnp.transpose(top_far)

    spread = proxies.reshape(6, leaves // 2, proxies.shape[2])
    geo_low = lax.ppermute(
        jnp.concatenate([geometry[:, leaves - reach :], spread], axis=2), AXES, forward
    )
    geo_high = lax.ppermute(
        jnp.concatenate([geometry[:, :reach], spread], axis=2), AXES, backward
    )
    den_low = lax.ppermute(density[:, (leaves - reach) * width :], AXES, forward)
    den_high = lax.ppermute(density[:, : reach * width], AXES, backward)
    sources = local(near_list, first, total)
    sources = jnp.where(sources < 0, sources + leaves + reach, sources)
    near_list = jnp.concatenate([sources, near_count[None]], axis=0)
    far_list = local(far_list, first, total) + leaves
    other_list = swap(near_list)
    geo_other = swap(geometry)
    den_other = swap(density)

    coefficients, partial = lift(density, bases, leaf_transfer, parent_transfer)

    count = lax.axis_size("sub")
    step = 1
    while step < count:
        partial = partial + lax.ppermute(partial, "sub", [(i, i ^ step) for i in range(count)])
        if step == 1:
            partial, geo_low, geo_high, other_list = lax.optimization_barrier(
                (partial, geo_low, geo_high, other_list)
            )
        step *= 2
    partial, den_low, den_high = lax.optimization_barrier((partial, den_low, den_high))
    coupled = partial.astype(jnp.bfloat16)[None]
    count = lax.axis_size("leaf")
    step = 1
    while step < count:
        other = lax.ppermute(coupled, "leaf", [(i, i ^ step) for i in range(count)])
        coupled = jnp.concatenate([coupled, other], axis=0)
        step *= 2

    coef_low = lax.ppermute(coefficients, AXES, forward)
    coef_high = lax.ppermute(coefficients, AXES, backward)
    geo_side = swap(jnp.where(side == 0, geo_high, geo_low))
    den_side = swap(jnp.where(side == 0, den_high, den_low))
    coupled, place = lax.optimization_barrier((coupled, place))
    near, near_other = near_field(
        place, (near_list, other_list),
        (geometry, geo_low, geo_high, geo_other, geo_side),
        (density, den_low, den_high, den_other, den_side),
    )
    near_other, coef_low, coef_high = lax.optimization_barrier((near_other, coef_low, coef_high))
    near_back = swap(near_other)
    return finish(
        place, far_list, top_far, top_proxies, coupled,
        (coefficients, coef_low, coef_high), (proxies, geo_low, geo_high),
        near, near_back, density, bases, leaf_transfer, parent_transfer,
    )


def solution(mesh):
    placed = (
        P(None, AXES),
        P(AXES, None, None),
        P(AXES, None),
        P(AXES),
        P(AXES, None),
        P(AXES, None, None),
        P(AXES, None, None),
        P(AXES, None, None),
        P(AXES, None, None),
        P(),
        P(),
    )
    return jax.shard_map(
        per_device, mesh=mesh, in_specs=placed, out_specs=P(None, AXES), check_vma=False
    )
```

profile of v0, /device:TPU:77, one launch (start us, length us, event | category | flops | bytes accessed | tf_op | source)
XLA Modules:
  0.0 134.0 jit_solution(8171337258057951967)
XLA Ops:
  0.0 1.0 fusion.1
  1.1 1.8 %pad_maximum_fusion = (f32[6,32,320]{2,1,0:T(8,128)}, f32[6,32,320]{2,1,0:T(8,128)}) fusion(f32[6,32,64]{2,1,0:T(8,128)} %bitcast.19, f32[6,32,256]{2,1,0:T(8,128)S(1)} %get-tuple-element.39, f32[6,32,256]{2,1,0:T(8,128)S(1)} %get-tuple-element.40), kind=kLoop, calls=%fused_computation.1 | loop fusion | flops 122880 | bytes 933888 | tf_op jit(solution)/shard_map/concatenate | solution.py:448
  2.8 1.3 collective-permute-start.1
  4.3 7.3 %shard_map.109 = (bf16[32,32,128]{2,1,0:T(8,128)(2,1)}, f32[32,64]{1,0:T(8,128)}) custom-call(bf16[32,16384]{1,0:T(8,128)(2,1)} %density.3, bf16[64,64,256]{2,1,0:T(8,128)(2,1)} %bases.3, bf16[64,64,64]{2,1,0:T(8,128)(2,1)} %leaf_transfer.3, bf16[8,64,64]{2,1,0:T(8,128)(2,1)} %parent_transfer.3), custom_call_target="tpu_custom_call" | custom-call | tf_op jit(solution)/shard_map/pallas_call | solution.py:55
  11.6 3.8 %collective-permute-start = (f32[32,64]{1,0:T(8,128)}, f32[32,64]{1,0:T(8,128)S(1)}, u32[]{:S(2)}, u32[]{:S(2)}) collective-permute-start(f32[32,64]{1,0:T(8,128)} %get-tuple-element.21), channel_id=1, source_target_pairs={{0,1},{1,0},{2,3},{3,2},{4,5},{5,4},{6,7},{7,6},{8,9},{9,8},{10,11... | collective-permute-start | bytes 24584 | tf_op jit(solution)/shard_map/ppermute | solution.py:465
  15.4 1.0 fusion
  16.4 1.5 %collective-permute-start.7 = (bf16[32,8192]{1,0:T(8,128)(2,1)}, bf16[32,8192]{1,0:T(8,128)(2,1)S(1)}, u32[]{:S(2)}, u32[]{:S(2)}) collective-permute-start(bf16[32,8192]{1,0:T(8,128)(2,1)} %get-tuple-element.37), channel_id=1, source_target_pairs={{1,0},{2,1},{3,2},{4,3},{5,4},{6,5},{7,6},{8,7},{9,8},{10,9},{11,1... | collective-permute-start | bytes 1572872 | tf_op jit(solution)/shard_map/ppermute | solution.py:451
  17.9 2.2 %collective-permute-start.3 = (s32[10,64]{1,0:T(8,128)S(1)}, s32[10,64]{1,0:T(8,128)S(1)}, u32[]{:S(2)}, u32[]{:S(2)}) collective-permute-start(s32[10,64]{1,0:T(8,128)S(1)} %pad_add_fusion.near_list), channel_id=1, source_target_pairs={{0,8},{8,0},{16,24},{24,16},{32,40},{40,32},{48,56},{56,48},{64,72... | collective-permute-start | bytes 7688 | tf_op jit(solution)/shard_map/ppermute | solution.py:431
  20.1 0.8 collective-permute-done.3.other_list
  21.4 1.4 %collective-permute-start.4 = (f32[32,64]{1,0:T(8,128)S(1)}, f32[32,64]{1,0:T(8,128)S(1)}, u32[]{:S(2)}, u32[]{:S(2)}) collective-permute-start(f32[32,64]{1,0:T(8,128)S(1)} %add.58), channel_id=1, source_target_pairs={{0,2},{1,3},{2,0},{3,1},{4,6},{5,7},{6,4},{7,5},{8,10},{9,11},{10,... | collective-permute-start | bytes 24584 | tf_op jit(solution)/shard_map/ppermute | solution.py:465
  22.9 9.3 %collective-permute-done.4 = f32[32,64]{1,0:T(8,128)S(1)} collective-permute-done((f32[32,64]{1,0:T(8,128)S(1)}, f32[32,64]{1,0:T(8,128)S(1)}, u32[]{:S(2)}, u32[]{:S(2)}) %collective-permute-start.4) | collective-permute-done | bytes 8224 | tf_op jit(solution)/shard_map/ppermute | solution.py:465
  32.2 4.0 %collective-permute-done.5 = f32[32,64]{1,0:T(8,128)S(1)} collective-permute-done((f32[32,64]{1,0:T(8,128)S(1)}, f32[32,64]{1,0:T(8,128)S(1)}, u32[]{:S(2)}, u32[]{:S(2)}) %collective-permute-start.5) | collective-permute-done | bytes 8224 | tf_op jit(solution)/shard_map/ppermute | solution.py:465
  36.5 0.4 collective-permute-start.8
  37.3 0.6 collective-permute-done.8
  37.9 2.7 %collective-permute-start.9 = (bf16[2,32,64]{2,1,0:T(8,128)(2,1)S(1)}, bf16[2,32,64]{2,1,0:T(8,128)(2,1)S(1)}, u32[]{:S(2)}, u32[]{:S(2)}) collective-permute-start(bf16[2,32,64]{2,1,0:T(8,128)(2,1)S(1)} %pad_maximum_fusion.4), channel_id=1, source_target_pairs={{0,16},{8,24},{16,0},{24,8},{32,48},{40,56},{48,32},{56,40},{64,80... | collective-permute-start | bytes 24584 | tf_op jit(solution)/shard_map/ppermute | solution.py:476
  40.6 1.1 collective-permute-done.9
  41.8 4.2 %collective-permute-done.10 = bf16[4,32,64]{2,1,0:T(8,128)(2,1)S(1)} collective-permute-done((bf16[4,32,64]{2,1,0:T(8,128)(2,1)S(1)}, bf16[4,32,64]{2,1,0:T(8,128)(2,1)S(1)}, u32[]{:S(2)}, u32[]{:S(2)}) %collective-permute-start.10) | collective-permute-done | bytes 16416 | tf_op jit(solution)/shard_map/ppermute | solution.py:476
  46.1 1.4 %collective-permute-start.11 = (bf16[8,32,64]{2,1,0:T(8,128)(2,1)S(1)}, bf16[8,32,64]{2,1,0:T(8,128)(2,1)S(1)}, u32[]{:S(2)}, u32[]{:S(2)}) collective-permute-start(bf16[8,32,64]{2,1,0:T(8,128)(2,1)S(1)} %pad_maximum_fusion.2), channel_id=1, source_target_pairs={{0,64},{8,72},{16,80},{24,88},{32,96},{40,104},{48,112},{56,120},{... | collective-permute-start | bytes 98312 | tf_op jit(solution)/shard_map/ppermute | solution.py:476
  47.4 1.8 %collective-permute-done.11 = bf16[8,32,64]{2,1,0:T(8,128)(2,1)S(1)} collective-permute-done((bf16[8,32,64]{2,1,0:T(8,128)(2,1)S(1)}, bf16[8,32,64]{2,1,0:T(8,128)(2,1)S(1)}, u32[]{:S(2)}, u32[]{:S(2)}) %collective-permute-start.11) | collective-permute-done | bytes 32800 | tf_op jit(solution)/shard_map/ppermute | solution.py:476
  49.4 1.5 %collective-permute-start.17 = (bf16[32,32,128]{2,1,0:T(8,128)(2,1)S(1)}, bf16[32,32,128]{2,1,0:T(8,128)(2,1)S(1)}, u32[]{:S(2)}, u32[]{:S(2)}) collective-permute-start(bf16[32,32,128]{2,1,0:T(8,128)(2,1)S(1)} %copy-done.5), channel_id=1, source_target_pairs={{1,0},{2,1},{3,2},{4,3},{5,4},{6,5},{7,6},{8,7},{9,8},{10,9},{11,1... | collective-permute-start | bytes 786440 | tf_op jit(solution)/shard_map/ppermute | solution.py:481
  50.9 57.5 %shard_map.110 = (f32[32,32,256]{2,1,0:T(8,128)S(1)}, bf16[32,32,256]{2,1,0:T(8,128)(2,1)S(1)}) custom-call(s32[2]{0:T(128)S(1)} %pad_add_fusion.1.place, s32[10,64]{1,0:T(8,128)S(1)} %pad_add_fusion.near_list, s32[10,64]{1,0:T(8,128)S(1)} %collective-permute-done.3.other_list, f32[6,64,256]{2,1,0:T(8,128)S(1)} %bitcast.23, ...), custom_call_target="tpu_custom_call" | custom-call | flops 49999998976 | bytes 8000000 | tf_op jit(solution)/shard_map/pallas_call | solution.py:262
  108.4 9.8 %collective-permute-start.18 = (bf16[32,32,256]{2,1,0:T(8,128)(2,1)S(1)}, bf16[32,32,256]{2,1,0:T(8,128)(2,1)S(1)}, u32[]{:S(2)}, u32[]{:S(2)}) collective-permute-start(bf16[32,32,256]{2,1,0:T(8,128)(2,1)S(1)} %get-tuple-element.36), channel_id=1, source_target_pairs={{0,8},{8,0},{16,24},{24,16},{32,40},{40,32},{48,56},{56,48},{64,72... | collective-permute-start | bytes 1572872 | tf_op jit(solution)/shard_map/ppermute | solution.py:431
  118.2 1.5 %collective-permute-done.18.near_back = bf16[32,32,256]{2,1,0:T(8,128)(2,1)S(1)} collective-permute-done((bf16[32,32,256]{2,1,0:T(8,128)(2,1)S(1)}, bf16[32,32,256]{2,1,0:T(8,128)(2,1)S(1)}, u32[]{:S(2)}, u32[]{:S(2)}) %collective-permute-start.18) | collective-permute-done | bytes 524320 | tf_op jit(solution)/shard_map/ppermute | solution.py:431
  119.8 14.3 %shard_map.111 = f32[32,16384]{1,0:T(8,128)} custom-call(s32[2]{0:T(128)S(1)} %pad_add_fusion.1.place, s32[16,64]{1,0:T(8,128)S(1)} %add_bitcast_fusion.far_list, s32[8,16]{1,0:T(8,128)S(1)} %bitcast.25, f32[3,16,64]{2,1,0:T(8,128)S(1)} %bitcast.24, bf16[16,32,64]{2,1,0:T(8,128)(2,1)S(1)} %constant_dynamic-update-slice_fusion.coupled, ...), custom_call_target="tpu_custom_call" | custom-call | tf_op jit(solution)/shard_map/pallas_call | solution.py:398
  (61 shorter events, 1.7 us)
Async XLA Ops:
  2.8 18.4 %collective-permute-start.1 = (f32[6,32,320]{2,1,0:T(8,128)}, f32[6,32,320]{2,1,0:T(8,128)S(1)}, u32[]{:S(2)}, u32[]{:S(2)}) collective-permute-start(f32[6,32,320]{2,1,0:T(8,128)} %get-tuple-element.42), channel_id=1, source_target_pairs={{0,1},{1,2},{2,3},{3,4},{4,5},{5,6},{6,7},{7,8},{8,9},{9,10},{10,1... | collective-permute-start | bytes 737288 | tf_op jit(solution)/shard_map/ppermute | solution.py:444
  4.1 17.3 %collective-permute-start.2 = (f32[6,32,320]{2,1,0:T(8,128)}, f32[6,32,320]{2,1,0:T(8,128)S(1)}, u32[]{:S(2)}, u32[]{:S(2)}) collective-permute-start(f32[6,32,320]{2,1,0:T(8,128)} %get-tuple-element.41), channel_id=1, source_target_pairs={{1,0},{2,1},{3,2},{4,3},{5,4},{6,5},{7,6},{8,7},{9,8},{10,9},{11,1... | collective-permute-start | bytes 737288 | tf_op jit(solution)/shard_map/ppermute | solution.py:447
  11.6 6.3 %collective-permute-start = (f32[32,64]{1,0:T(8,128)}, f32[32,64]{1,0:T(8,128)S(1)}, u32[]{:S(2)}, u32[]{:S(2)}) collective-permute-start(f32[32,64]{1,0:T(8,128)} %get-tuple-element.21), channel_id=1, source_target_pairs={{0,1},{1,0},{2,3},{3,2},{4,5},{5,4},{6,7},{7,6},{8,9},{9,8},{10,11... | collective-permute-start | bytes 24584 | tf_op jit(solution)/shard_map/ppermute | solution.py:465
  16.4 20.1 %collective-permute-start.6 = (bf16[32,8192]{1,0:T(8,128)(2,1)}, bf16[32,8192]{1,0:T(8,128)(2,1)S(1)}, u32[]{:S(2)}, u32[]{:S(2)}) collective-permute-start(bf16[32,8192]{1,0:T(8,128)(2,1)} %get-tuple-element.38), channel_id=1, source_target_pairs={{0,1},{1,2},{2,3},{3,4},{4,5},{5,6},{6,7},{7,8},{8,9},{9,10},{10,1... | collective-permute-start | bytes 1572872 | tf_op jit(solution)/shard_map/ppermute | solution.py:450
  16.4 20.1 %collective-permute-start.7 = (bf16[32,8192]{1,0:T(8,128)(2,1)}, bf16[32,8192]{1,0:T(8,128)(2,1)S(1)}, u32[]{:S(2)}, u32[]{:S(2)}) collective-permute-start(bf16[32,8192]{1,0:T(8,128)(2,1)} %get-tuple-element.37), channel_id=1, source_target_pairs={{1,0},{2,1},{3,2},{4,3},{5,4},{6,5},{7,6},{8,7},{9,8},{10,9},{11,1... | collective-permute-start | bytes 1572872 | tf_op jit(solution)/shard_map/ppermute | solution.py:451
  17.9 3.0 %collective-permute-start.3 = (s32[10,64]{1,0:T(8,128)S(1)}, s32[10,64]{1,0:T(8,128)S(1)}, u32[]{:S(2)}, u32[]{:S(2)}) collective-permute-start(s32[10,64]{1,0:T(8,128)S(1)} %pad_add_fusion.near_list), channel_id=1, source_target_pairs={{0,8},{8,0},{16,24},{24,16},{32,40},{40,32},{48,56},{56,48},{64,72... | collective-permute-start | bytes 7688 | tf_op jit(solution)/shard_map/ppermute | solution.py:431
  20.9 28.5 %collective-permute-start.12 = (f32[6,64,256]{2,1,0:T(8,128)S(1)}, f32[6,64,256]{2,1,0:T(8,128)}, u32[]{:S(2)}, u32[]{:S(2)}) collective-permute-start(f32[6,64,256]{2,1,0:T(8,128)S(1)} %bitcast.22), channel_id=1, source_target_pairs={{0,8},{8,0},{16,24},{24,16},{32,40},{40,32},{48,56},{56,48},{64,72... | collective-permute-start | bytes 1179656 | tf_op jit(solution)/shard_map/ppermute | solution.py:431
  21.3 29.7 %collective-permute-start.14 = (bf16[32,16384]{1,0:T(8,128)(2,1)S(1)}, bf16[32,16384]{1,0:T(8,128)(2,1)}, u32[]{:S(2)}, u32[]{:S(2)}) collective-permute-start(bf16[32,16384]{1,0:T(8,128)(2,1)S(1)} %copy-done), channel_id=1, source_target_pairs={{0,8},{8,0},{16,24},{24,16},{32,40},{40,32},{48,56},{56,48},{64,72... | collective-permute-start | bytes 3145736 | tf_op jit(solution)/shard_map/ppermute | solution.py:431
  21.4 10.7 %collective-permute-start.4 = (f32[32,64]{1,0:T(8,128)S(1)}, f32[32,64]{1,0:T(8,128)S(1)}, u32[]{:S(2)}, u32[]{:S(2)}) collective-permute-start(f32[32,64]{1,0:T(8,128)S(1)} %add.58), channel_id=1, source_target_pairs={{0,2},{1,3},{2,0},{3,1},{4,6},{5,7},{6,4},{7,5},{8,10},{9,11},{10,... | collective-permute-start | bytes 24584 | tf_op jit(solution)/shard_map/ppermute | solution.py:465
  32.2 4.1 %collective-permute-start.5 = (f32[32,64]{1,0:T(8,128)S(1)}, f32[32,64]{1,0:T(8,128)S(1)}, u32[]{:S(2)}, u32[]{:S(2)}) collective-permute-start(f32[32,64]{1,0:T(8,128)S(1)} %add.65), channel_id=1, source_target_pairs={{0,4},{1,5},{2,6},{3,7},{4,0},{5,1},{6,2},{7,3},{8,12},{9,13},{10,... | collective-permute-start | bytes 24584 | tf_op jit(solution)/shard_map/ppermute | solution.py:465
  36.3 14.7 %collective-permute-start.13 = (f32[6,32,320]{2,1,0:T(8,128)S(1)}, f32[6,32,320]{2,1,0:T(8,128)S(1)}, u32[]{:S(2)}, u32[]{:S(2)}) collective-permute-start(f32[6,32,320]{2,1,0:T(8,128)S(1)} %broadcast_select_fusion.1), channel_id=1, source_target_pairs={{0,8},{8,0},{16,24},{24,16},{32,40},{40,32},{48,56},{56,48},{64,72... | collective-permute-start | bytes 737288 | tf_op jit(solution)/shard_map/ppermute | solution.py:431
  36.5 1.3 %collective-permute-start.8 = (bf16[1,32,64]{2,1,0:T(8,128)(2,1)S(1)}, bf16[1,32,64]{2,1,0:T(8,128)(2,1)S(1)}, u32[]{:S(2)}, u32[]{:S(2)}) collective-permute-start(bf16[1,32,64]{2,1,0:T(8,128)(2,1)S(1)} %bitcast.26), channel_id=1, source_target_pairs={{0,8},{8,0},{16,24},{24,16},{32,40},{40,32},{48,56},{56,48},{64,72... | collective-permute-start | bytes 12296 | tf_op jit(solution)/shard_map/ppermute | solution.py:476
  36.9 14.0 %collective-permute-start.15 = (bf16[32,8192]{1,0:T(8,128)(2,1)S(1)}, bf16[32,8192]{1,0:T(8,128)(2,1)S(1)}, u32[]{:S(2)}, u32[]{:S(2)}) collective-permute-start(bf16[32,8192]{1,0:T(8,128)(2,1)S(1)} %broadcast_select_fusion), channel_id=1, source_target_pairs={{0,8},{8,0},{16,24},{24,16},{32,40},{40,32},{48,56},{56,48},{64,72... | collective-permute-start | bytes 1572872 | tf_op jit(solution)/shard_map/ppermute | solution.py:431
  37.9 3.8 %collective-permute-start.9 = (bf16[2,32,64]{2,1,0:T(8,128)(2,1)S(1)}, bf16[2,32,64]{2,1,0:T(8,128)(2,1)S(1)}, u32[]{:S(2)}, u32[]{:S(2)}) collective-permute-start(bf16[2,32,64]{2,1,0:T(8,128)(2,1)S(1)} %pad_maximum_fusion.4), channel_id=1, source_target_pairs={{0,16},{8,24},{16,0},{24,8},{32,48},{40,56},{48,32},{56,40},{64,80... | collective-permute-start | bytes 24584 | tf_op jit(solution)/shard_map/ppermute | solution.py:476
  41.7 4.3 %collective-permute-start.10 = (bf16[4,32,64]{2,1,0:T(8,128)(2,1)S(1)}, bf16[4,32,64]{2,1,0:T(8,128)(2,1)S(1)}, u32[]{:S(2)}, u32[]{:S(2)}) collective-permute-start(bf16[4,32,64]{2,1,0:T(8,128)(2,1)S(1)} %pad_maximum_fusion.3), channel_id=1, source_target_pairs={{0,32},{8,40},{16,48},{24,56},{32,0},{40,8},{48,16},{56,24},{64,96... | collective-permute-start | bytes 49160 | tf_op jit(solution)/shard_map/ppermute | solution.py:476
  46.1 3.2 %collective-permute-start.11 = (bf16[8,32,64]{2,1,0:T(8,128)(2,1)S(1)}, bf16[8,32,64]{2,1,0:T(8,128)(2,1)S(1)}, u32[]{:S(2)}, u32[]{:S(2)}) collective-permute-start(bf16[8,32,64]{2,1,0:T(8,128)(2,1)S(1)} %pad_maximum_fusion.2), channel_id=1, source_target_pairs={{0,64},{8,72},{16,80},{24,88},{32,96},{40,104},{48,112},{56,120},{... | collective-permute-start | bytes 98312 | tf_op jit(solution)/shard_map/ppermute | solution.py:476
  49.3 59.1 %collective-permute-start.16 = (bf16[32,32,128]{2,1,0:T(8,128)(2,1)S(1)}, bf16[32,32,128]{2,1,0:T(8,128)(2,1)S(1)}, u32[]{:S(2)}, u32[]{:S(2)}) collective-permute-start(bf16[32,32,128]{2,1,0:T(8,128)(2,1)S(1)} %copy-done.5), channel_id=1, source_target_pairs={{0,1},{1,2},{2,3},{3,4},{4,5},{5,6},{6,7},{7,8},{8,9},{9,10},{10,1... | collective-permute-start | bytes 786440 | tf_op jit(solution)/shard_map/ppermute | solution.py:480
  49.3 70.4 %copy-start.1 = (bf16[64,64,64]{2,1,0:T(8,128)(2,1)S(1)}, bf16[64,64,64]{2,1,0:T(8,128)(2,1)}, u32[]{:S(2)}) copy-start(bf16[64,64,64]{2,1,0:T(8,128)(2,1)} %leaf_transfer.3) | copy-start | bytes 1572868
  49.3 70.4 %copy-start.2 = (bf16[8,64,64]{2,1,0:T(8,128)(2,1)S(1)}, bf16[8,64,64]{2,1,0:T(8,128)(2,1)}, u32[]{:S(2)}) copy-start(bf16[8,64,64]{2,1,0:T(8,128)(2,1)} %parent_transfer.3) | copy-start | bytes 196612
  49.3 70.4 %copy-start.3 = (f32[64,3,64]{2,0,1:T(8,128)S(1)}, f32[64,3,64]{2,0,1:T(8,128)}, u32[]{:S(2)}) copy-start(f32[64,3,64]{2,0,1:T(8,128)} %param.17) | copy-start | bytes 147460
  49.4 70.4 %copy-start.6 = (f32[16,3,64]{2,0,1:T(8,128)S(1)}, f32[16,3,64]{2,0,1:T(8,128)}, u32[]{:S(2)}) copy-start(f32[16,3,64]{2,0,1:T(8,128)} %param.20) | copy-start | bytes 36868
  49.4 70.4 %copy-start.7 = (s32[16,8]{0,1:T(8,128)S(1)}, s32[16,8]{0,1:T(8,128)}, u32[]{:S(2)}) copy-start(s32[16,8]{0,1:T(8,128)} %param.21) | copy-start | bytes 1540
  49.4 59.0 %collective-permute-start.17 = (bf16[32,32,128]{2,1,0:T(8,128)(2,1)S(1)}, bf16[32,32,128]{2,1,0:T(8,128)(2,1)S(1)}, u32[]{:S(2)}, u32[]{:S(2)}) collective-permute-start(bf16[32,32,128]{2,1,0:T(8,128)(2,1)S(1)} %copy-done.5), channel_id=1, source_target_pairs={{1,0},{2,1},{3,2},{4,3},{5,4},{6,5},{7,6},{8,7},{9,8},{10,9},{11,1... | collective-permute-start | bytes 786440 | tf_op jit(solution)/shard_map/ppermute | solution.py:481
  108.4 11.3 %collective-permute-start.18 = (bf16[32,32,256]{2,1,0:T(8,128)(2,1)S(1)}, bf16[32,32,256]{2,1,0:T(8,128)(2,1)S(1)}, u32[]{:S(2)}, u32[]{:S(2)}) collective-permute-start(bf16[32,32,256]{2,1,0:T(8,128)(2,1)S(1)} %get-tuple-element.36), channel_id=1, source_target_pairs={{0,8},{8,0},{16,24},{24,16},{32,40},{40,32},{48,56},{56,48},{64,72... | collective-permute-start | bytes 1572872 | tf_op jit(solution)/shard_map/ppermute | solution.py:431
  (7 other events, 148.3 us)
where the time goes:
time: 134 us
  Pallas kernels  79 us (59%)
  starting transfers between devices  27.1 us (20%)
  waiting for transfers between devices  23.5 us (18%)
  local copies, waits for them, and re-layouts  2.18 us (2%)
  other arithmetic  2 us (1%)
    pallas_call x1, Pallas kernels, near_field(): pl.pallas_call(near_kernel, out_shape=(jax.ShapeDtypeStruct(half, jnp.flo...  57.5 us
    pallas_call x1, Pallas kernels, finish(): pl.pallas_call(final_kernel, out_shape=jax.ShapeDtypeStruct(density.shape...  14.3 us
    ppermute x3, waiting for transfers between devices, per_device(): lax.ppermute(partial, 'sub', [(i, i ^ step) for i in range(count)])  13.4 us
    ppermute x6, starting transfers between devices, swap(): return lax.ppermute(value, 'leaf', [(i, i ^ 1) for i in range(groups)])  13 us
    ppermute x4, waiting for transfers between devices, per_device(): other = lax.ppermute(coupled, 'leaf', [(i, i ^ step) for i in range(count)])  7.8 us
    pallas_call x1, Pallas kernels, lift(): pl.pallas_call(lift_kernel, grid=(parents,), out_shape=(jax.ShapeDtypeStr...  7.28 us
    ppermute x3, starting transfers between devices, per_device(): lax.ppermute(partial, 'sub', [(i, i ^ step) for i in range(count)])  5.14 us
    ppermute x4, starting transfers between devices, per_device(): other = lax.ppermute(coupled, 'leaf', [(i, i ^ step) for i in range(count)])  4.5 us
  transfers between devices with their start and end apart: 19, of which 8 were waited for; matrix products, arithmetic and copies ran while one was open for 1% of the time, Pallas kernels for 48%

commit v1 on v0

--- a/solution.py
+++ b/solution.py
@@ -468,26 +468,30 @@
                 (partial, geo_low, geo_high, other_list)
             )
         step *= 2
-    partial, den_low, den_high = lax.optimization_barrier((partial, den_low, den_high))
     coupled = partial.astype(jnp.bfloat16)[None]
     count = lax.axis_size("leaf")
     step = 1
     while step < count:
+        if 2 * step == count:
+            coupled, place = lax.optimization_barrier((coupled, place))
         other = lax.ppermute(coupled, "leaf", [(i, i ^ step) for i in range(count)])
         coupled = jnp.concatenate([coupled, other], axis=0)
+        if step == 2:
+            coupled, den_low, den_high = lax.optimization_barrier((coupled, den_low, den_high))
         step *= 2
 
     coef_low = lax.ppermute(coefficients, AXES, forward)
     coef_high = lax.ppermute(coefficients, AXES, backward)
     geo_side = swap(jnp.where(side == 0, geo_high, geo_low))
     den_side = swap(jnp.where(side == 0, den_high, den_low))
-    coupled, place = lax.optimization_barrier((coupled, place))
     near, near_other = near_field(
         place, (near_list, other_list),
         (geometry, geo_low, geo_high, geo_other, geo_side),
         (density, den_low, den_high, den_other, den_side),
     )
-    near_other, coef_low, coef_high = lax.optimization_barrier((near_other, coef_low, coef_high))
+    near_other, coef_low, coef_high, coupled = lax.optimization_barrier(
+        (near_other, coef_low, coef_high, coupled)
+    )
     near_back = swap(near_other)
     return finish(
         place, far_list, top_far, top_proxies, coupled,

time: 134 us -> 133 us (level)
  the two profiles are of different devices: /device:TPU:77 before, /device:TPU:71 now
where the time goes in v1:
time: 133 us; the launch traced here: 135 us
  Pallas kernels  80.2 us (60%)
  starting transfers between devices  31.9 us (24%)
  waiting for transfers between devices  18.8 us (14%)
  local copies, waits for them, and re-layouts  2.14 us (2%)
  other arithmetic  2.02 us (2%)
    pallas_call x1, Pallas kernels, near_field(): pl.pallas_call(near_kernel, out_shape=(jax.ShapeDtypeStruct(half, jnp.flo...  58.7 us
    pallas_call x1, Pallas kernels, finish(): pl.pallas_call(final_kernel, out_shape=jax.ShapeDtypeStruct(density.shape...  14.3 us
    ppermute x6, starting transfers between devices, swap(): return lax.ppermute(value, 'leaf', [(i, i ^ 1) for i in range(groups)])  10.4 us
    ppermute x4, waiting for transfers between devices, per_device(): other = lax.ppermute(coupled, 'leaf', [(i, i ^ step) for i in range(count)])  8.6 us
    ppermute x3, waiting for transfers between devices, per_device(): lax.ppermute(partial, 'sub', [(i, i ^ step) for i in range(count)])  7.86 us
    pallas_call x1, Pallas kernels, lift(): pl.pallas_call(lift_kernel, grid=(parents,), out_shape=(jax.ShapeDtypeStr...  7.19 us
    ppermute x4, starting transfers between devices, per_device(): other = lax.ppermute(coupled, 'leaf', [(i, i ^ step) for i in range(count)])  4.28 us
    ppermute x1, starting transfers between devices, per_device(): lax.ppermute(jnp.concatenate([geometry[:, :reach], spread], axis=2), AXES...  3.78 us
  transfers between devices with their start and end apart: 19, of which 8 were waited for; matrix products, arithmetic and copies ran while one was open for 1% of the time, Pallas kernels for 49%

profile of v1, /device:TPU:71, one launch (start us, length us, event | category | flops | bytes accessed | tf_op | source)
XLA Modules:
  0.0 135.4 jit_solution(4687662643895560423)
XLA Ops:
  0.0 1.0 fusion.2
  1.1 1.8 %pad_maximum_fusion = (f32[6,32,320]{2,1,0:T(8,128)}, f32[6,32,320]{2,1,0:T(8,128)}) fusion(f32[6,32,64]{2,1,0:T(8,128)} %bitcast.17, f32[6,32,256]{2,1,0:T(8,128)S(1)} %get-tuple-element.41, f32[6,32,256]{2,1,0:T(8,128)S(1)} %get-tuple-element.42), kind=kLoop, calls=%fused_computation.1 | loop fusion | flops 122880 | bytes 933888 | tf_op jit(solution)/shard_map/concatenate | solution.py:448
  2.8 1.3 collective-permute-start.1
  4.1 3.8 %collective-permute-start.2 = (f32[6,32,320]{2,1,0:T(8,128)}, f32[6,32,320]{2,1,0:T(8,128)S(1)}, u32[]{:S(2)}, u32[]{:S(2)}) collective-permute-start(f32[6,32,320]{2,1,0:T(8,128)} %get-tuple-element.43), channel_id=1, source_target_pairs={{1,0},{2,1},{3,2},{4,3},{5,4},{6,5},{7,6},{8,7},{9,8},{10,9},{11,1... | collective-permute-start | bytes 737288 | tf_op jit(solution)/shard_map/ppermute | solution.py:447
  7.9 7.2 %shard_map.109 = (bf16[32,32,128]{2,1,0:T(8,128)(2,1)}, f32[32,64]{1,0:T(8,128)}) custom-call(bf16[32,16384]{1,0:T(8,128)(2,1)} %density.3, bf16[64,64,256]{2,1,0:T(8,128)(2,1)} %bases.3, bf16[64,64,64]{2,1,0:T(8,128)(2,1)} %leaf_transfer.3, bf16[8,64,64]{2,1,0:T(8,128)(2,1)} %parent_transfer.3), custom_call_target="tpu_custom_call" | custom-call | tf_op jit(solution)/shard_map/pallas_call | solution.py:55
  15.2 1.0 fusion.1
  16.3 1.4 %collective-permute-start.8 = (bf16[32,8192]{1,0:T(8,128)(2,1)}, bf16[32,8192]{1,0:T(8,128)(2,1)S(1)}, u32[]{:S(2)}, u32[]{:S(2)}) collective-permute-start(bf16[32,8192]{1,0:T(8,128)(2,1)} %get-tuple-element.40), channel_id=1, source_target_pairs={{0,1},{1,2},{2,3},{3,4},{4,5},{5,6},{6,7},{7,8},{8,9},{9,10},{10,1... | collective-permute-start | bytes 1572872 | tf_op jit(solution)/shard_map/ppermute | solution.py:450
  17.7 3.6 %collective-permute-start.9 = (bf16[32,8192]{1,0:T(8,128)(2,1)}, bf16[32,8192]{1,0:T(8,128)(2,1)S(1)}, u32[]{:S(2)}, u32[]{:S(2)}) collective-permute-start(bf16[32,8192]{1,0:T(8,128)(2,1)} %get-tuple-element.39), channel_id=1, source_target_pairs={{1,0},{2,1},{3,2},{4,3},{5,4},{6,5},{7,6},{8,7},{9,8},{10,9},{11,1... | collective-permute-start | bytes 1572872 | tf_op jit(solution)/shard_map/ppermute | solution.py:451
  21.4 1.9 %collective-permute-start.3 = (s32[10,64]{1,0:T(8,128)S(1)}, s32[10,64]{1,0:T(8,128)S(1)}, u32[]{:S(2)}, u32[]{:S(2)}) collective-permute-start(s32[10,64]{1,0:T(8,128)S(1)} %pad_add_fusion.near_list), channel_id=1, source_target_pairs={{0,8},{8,0},{16,24},{24,16},{32,40},{40,32},{48,56},{56,48},{64,72... | collective-permute-start | bytes 7688 | tf_op jit(solution)/shard_map/ppermute | solution.py:431
  24.1 5.1 %collective-permute-done.4 = f32[32,64]{1,0:T(8,128)S(1)} collective-permute-done((f32[32,64]{1,0:T(8,128)S(1)}, f32[32,64]{1,0:T(8,128)S(1)}, u32[]{:S(2)}, u32[]{:S(2)}) %collective-permute-start.4) | collective-permute-done | bytes 8224 | tf_op jit(solution)/shard_map/ppermute | solution.py:465
  29.2 1.9 %collective-permute-start.5 = (f32[32,64]{1,0:T(8,128)S(1)}, f32[32,64]{1,0:T(8,128)S(1)}, u32[]{:S(2)}, u32[]{:S(2)}) collective-permute-start(f32[32,64]{1,0:T(8,128)S(1)} %add.65), channel_id=1, source_target_pairs={{0,4},{1,5},{2,6},{3,7},{4,0},{5,1},{6,2},{7,3},{8,12},{9,13},{10,... | collective-permute-start | bytes 24584 | tf_op jit(solution)/shard_map/ppermute | solution.py:465
  31.1 2.7 %collective-permute-done.5 = f32[32,64]{1,0:T(8,128)S(1)} collective-permute-done((f32[32,64]{1,0:T(8,128)S(1)}, f32[32,64]{1,0:T(8,128)S(1)}, u32[]{:S(2)}, u32[]{:S(2)}) %collective-permute-start.5) | collective-permute-done | bytes 8224 | tf_op jit(solution)/shard_map/ppermute | solution.py:465
  33.8 2.8 %collective-permute-start.6 = (bf16[1,32,64]{2,1,0:T(8,128)(2,1)S(1)}, bf16[1,32,64]{2,1,0:T(8,128)(2,1)S(1)}, u32[]{:S(2)}, u32[]{:S(2)}) collective-permute-start(bf16[1,32,64]{2,1,0:T(8,128)(2,1)S(1)} %fusion), channel_id=1, source_target_pairs={{0,8},{8,0},{16,24},{24,16},{32,40},{40,32},{48,56},{56,48},{64,72... | collective-permute-start | bytes 12296 | tf_op jit(solution)/shard_map/ppermute | solution.py:477
  36.6 0.8 collective-permute-done.6
  37.5 1.3 collective-permute-start.7
  40.2 1.6 %collective-permute-start.14 = (bf16[32,8192]{1,0:T(8,128)(2,1)S(1)}, bf16[32,8192]{1,0:T(8,128)(2,1)S(1)}, u32[]{:S(2)}, u32[]{:S(2)}) collective-permute-start(bf16[32,8192]{1,0:T(8,128)(2,1)S(1)} %broadcast_select_fusion), channel_id=1, source_target_pairs={{0,8},{8,0},{16,24},{24,16},{32,40},{40,32},{48,56},{56,48},{64,72... | collective-permute-start | bytes 1572872 | tf_op jit(solution)/shard_map/ppermute | solution.py:431
  42.1 4.1 %collective-permute-done.10 = bf16[4,32,64]{2,1,0:T(8,128)(2,1)S(1)} collective-permute-done((bf16[4,32,64]{2,1,0:T(8,128)(2,1)S(1)}, bf16[4,32,64]{2,1,0:T(8,128)(2,1)S(1)}, u32[]{:S(2)}, u32[]{:S(2)}) %collective-permute-start.10) | collective-permute-done | bytes 16416 | tf_op jit(solution)/shard_map/ppermute | solution.py:477
  46.3 3.0 %collective-permute-done.17 = bf16[8,32,64]{2,1,0:T(8,128)(2,1)S(1)} collective-permute-done((bf16[8,32,64]{2,1,0:T(8,128)(2,1)S(1)}, bf16[8,32,64]{2,1,0:T(8,128)(2,1)S(1)}, u32[]{:S(2)}, u32[]{:S(2)}) %collective-permute-start.17) | collective-permute-done | bytes 32800 | tf_op jit(solution)/shard_map/ppermute | solution.py:477
  49.4 2.5 %collective-permute-start.15 = (bf16[32,32,128]{2,1,0:T(8,128)(2,1)S(1)}, bf16[32,32,128]{2,1,0:T(8,128)(2,1)S(1)}, u32[]{:S(2)}, u32[]{:S(2)}) collective-permute-start(bf16[32,32,128]{2,1,0:T(8,128)(2,1)S(1)} %copy-done.5), channel_id=1, source_target_pairs={{0,1},{1,2},{2,3},{3,4},{4,5},{5,6},{6,7},{7,8},{8,9},{9,10},{10,1... | collective-permute-start | bytes 786440 | tf_op jit(solution)/shard_map/ppermute | solution.py:483
  52.0 2.7 %collective-permute-start.16 = (bf16[32,32,128]{2,1,0:T(8,128)(2,1)S(1)}, bf16[32,32,128]{2,1,0:T(8,128)(2,1)S(1)}, u32[]{:S(2)}, u32[]{:S(2)}) collective-permute-start(bf16[32,32,128]{2,1,0:T(8,128)(2,1)S(1)} %copy-done.5), channel_id=1, source_target_pairs={{1,0},{2,1},{3,2},{4,3},{5,4},{6,5},{7,6},{8,7},{9,8},{10,9},{11,1... | collective-permute-start | bytes 786440 | tf_op jit(solution)/shard_map/ppermute | solution.py:484
  54.7 58.7 %shard_map.110 = (f32[32,32,256]{2,1,0:T(8,128)S(1)}, bf16[32,32,256]{2,1,0:T(8,128)(2,1)S(1)}) custom-call(s32[2]{0:T(128)S(1)} %pad_add_fusion.1.place, s32[10,64]{1,0:T(8,128)S(1)} %pad_add_fusion.near_list, s32[10,64]{1,0:T(8,128)S(1)} %collective-permute-done.3.other_list, f32[6,64,256]{2,1,0:T(8,128)S(1)} %bitcast.21, ...), custom_call_target="tpu_custom_call" | custom-call | flops 49999998976 | bytes 8000000 | tf_op jit(solution)/shard_map/pallas_call | solution.py:262
  113.4 6.1 %collective-permute-start.18 = (bf16[32,32,256]{2,1,0:T(8,128)(2,1)S(1)}, bf16[32,32,256]{2,1,0:T(8,128)(2,1)S(1)}, u32[]{:S(2)}, u32[]{:S(2)}) collective-permute-start(bf16[32,32,256]{2,1,0:T(8,128)(2,1)S(1)} %get-tuple-element.38), channel_id=1, source_target_pairs={{0,8},{8,0},{16,24},{24,16},{32,40},{40,32},{48,56},{56,48},{64,72... | collective-permute-start | bytes 1572872 | tf_op jit(solution)/shard_map/ppermute | solution.py:431
  119.5 1.5 %collective-permute-done.18.near_back = bf16[32,32,256]{2,1,0:T(8,128)(2,1)S(1)} collective-permute-done((bf16[32,32,256]{2,1,0:T(8,128)(2,1)S(1)}, bf16[32,32,256]{2,1,0:T(8,128)(2,1)S(1)}, u32[]{:S(2)}, u32[]{:S(2)}) %collective-permute-start.18) | collective-permute-done | bytes 524320 | tf_op jit(solution)/shard_map/ppermute | solution.py:431
  121.1 14.3 %shard_map.111 = f32[32,16384]{1,0:T(8,128)} custom-call(s32[2]{0:T(128)S(1)} %pad_add_fusion.1.place, s32[16,64]{1,0:T(8,128)S(1)} %add_bitcast_fusion.far_list, s32[8,16]{1,0:T(8,128)S(1)} %bitcast.23, f32[3,16,64]{2,1,0:T(8,128)S(1)} %bitcast.22, bf16[16,32,64]{2,1,0:T(8,128)(2,1)S(1)} %pad_maximum_fusion.2.coupled, bf16[32,32,128]{2,1,0:T(8,128)(2,1)S(1)} %copy-done.5, ...), custom_call_target="tpu_custom_call" | custom-call | tf_op jit(solution)/shard_map/pallas_call | solution.py:398
  (57 shorter events, 2.8 us)
Async XLA Ops:
  2.8 21.3 %collective-permute-start.1 = (f32[6,32,320]{2,1,0:T(8,128)}, f32[6,32,320]{2,1,0:T(8,128)S(1)}, u32[]{:S(2)}, u32[]{:S(2)}) collective-permute-start(f32[6,32,320]{2,1,0:T(8,128)} %get-tuple-element.44), channel_id=1, source_target_pairs={{0,1},{1,2},{2,3},{3,4},{4,5},{5,6},{6,7},{7,8},{8,9},{9,10},{10,1... | collective-permute-start | bytes 737288 | tf_op jit(solution)/shard_map/ppermute | solution.py:444
  4.1 20.0 %collective-permute-start.2 = (f32[6,32,320]{2,1,0:T(8,128)}, f32[6,32,320]{2,1,0:T(8,128)S(1)}, u32[]{:S(2)}, u32[]{:S(2)}) collective-permute-start(f32[6,32,320]{2,1,0:T(8,128)} %get-tuple-element.43), channel_id=1, source_target_pairs={{1,0},{2,1},{3,2},{4,3},{5,4},{6,5},{7,6},{8,7},{9,8},{10,9},{11,1... | collective-permute-start | bytes 737288 | tf_op jit(solution)/shard_map/ppermute | solution.py:447
  15.1 6.2 %collective-permute-start = (f32[32,64]{1,0:T(8,128)}, f32[32,64]{1,0:T(8,128)S(1)}, u32[]{:S(2)}, u32[]{:S(2)}) collective-permute-start(f32[32,64]{1,0:T(8,128)} %get-tuple-element.22), channel_id=1, source_target_pairs={{0,1},{1,0},{2,3},{3,2},{4,5},{5,4},{6,7},{7,6},{8,9},{9,8},{10,11... | collective-permute-start | bytes 24584 | tf_op jit(solution)/shard_map/ppermute | solution.py:465
  16.3 23.9 %collective-permute-start.8 = (bf16[32,8192]{1,0:T(8,128)(2,1)}, bf16[32,8192]{1,0:T(8,128)(2,1)S(1)}, u32[]{:S(2)}, u32[]{:S(2)}) collective-permute-start(bf16[32,8192]{1,0:T(8,128)(2,1)} %get-tuple-element.40), channel_id=1, source_target_pairs={{0,1},{1,2},{2,3},{3,4},{4,5},{5,6},{6,7},{7,8},{8,9},{9,10},{10,1... | collective-permute-start | bytes 1572872 | tf_op jit(solution)/shard_map/ppermute | solution.py:450
  17.7 22.4 %collective-permute-start.9 = (bf16[32,8192]{1,0:T(8,128)(2,1)}, bf16[32,8192]{1,0:T(8,128)(2,1)S(1)}, u32[]{:S(2)}, u32[]{:S(2)}) collective-permute-start(bf16[32,8192]{1,0:T(8,128)(2,1)} %get-tuple-element.39), channel_id=1, source_target_pairs={{1,0},{2,1},{3,2},{4,3},{5,4},{6,5},{7,6},{8,7},{9,8},{10,9},{11,1... | collective-permute-start | bytes 1572872 | tf_op jit(solution)/shard_map/ppermute | solution.py:451
  21.4 2.7 %collective-permute-start.3 = (s32[10,64]{1,0:T(8,128)S(1)}, s32[10,64]{1,0:T(8,128)S(1)}, u32[]{:S(2)}, u32[]{:S(2)}) collective-permute-start(s32[10,64]{1,0:T(8,128)S(1)} %pad_add_fusion.near_list), channel_id=1, source_target_pairs={{0,8},{8,0},{16,24},{24,16},{32,40},{40,32},{48,56},{56,48},{64,72... | collective-permute-start | bytes 7688 | tf_op jit(solution)/shard_map/ppermute | solution.py:431
  24.1 5.1 %collective-permute-start.4 = (f32[32,64]{1,0:T(8,128)S(1)}, f32[32,64]{1,0:T(8,128)S(1)}, u32[]{:S(2)}, u32[]{:S(2)}) collective-permute-start(f32[32,64]{1,0:T(8,128)S(1)} %add.58), channel_id=1, source_target_pairs={{0,2},{1,3},{2,0},{3,1},{4,6},{5,7},{6,4},{7,5},{8,10},{9,11},{10,... | collective-permute-start | bytes 24584 | tf_op jit(solution)/shard_map/ppermute | solution.py:465
  29.2 4.6 %collective-permute-start.5 = (f32[32,64]{1,0:T(8,128)S(1)}, f32[32,64]{1,0:T(8,128)S(1)}, u32[]{:S(2)}, u32[]{:S(2)}) collective-permute-start(f32[32,64]{1,0:T(8,128)S(1)} %add.65), channel_id=1, source_target_pairs={{0,4},{1,5},{2,6},{3,7},{4,0},{5,1},{6,2},{7,3},{8,12},{9,13},{10,... | collective-permute-start | bytes 24584 | tf_op jit(solution)/shard_map/ppermute | solution.py:465
  33.8 3.6 %collective-permute-start.6 = (bf16[1,32,64]{2,1,0:T(8,128)(2,1)S(1)}, bf16[1,32,64]{2,1,0:T(8,128)(2,1)S(1)}, u32[]{:S(2)}, u32[]{:S(2)}) collective-permute-start(bf16[1,32,64]{2,1,0:T(8,128)(2,1)S(1)} %fusion), channel_id=1, source_target_pairs={{0,8},{8,0},{16,24},{24,16},{32,40},{40,32},{48,56},{56,48},{64,72... | collective-permute-start | bytes 12296 | tf_op jit(solution)/shard_map/ppermute | solution.py:477
  37.5 2.6 %collective-permute-start.7 = (bf16[2,32,64]{2,1,0:T(8,128)(2,1)S(1)}, bf16[2,32,64]{2,1,0:T(8,128)(2,1)S(1)}, u32[]{:S(2)}, u32[]{:S(2)}) collective-permute-start(bf16[2,32,64]{2,1,0:T(8,128)(2,1)S(1)} %pad_maximum_fusion.5), channel_id=1, source_target_pairs={{0,16},{8,24},{16,0},{24,8},{32,48},{40,56},{48,32},{56,40},{64,80... | collective-permute-start | bytes 24584 | tf_op jit(solution)/shard_map/ppermute | solution.py:477
  38.8 13.2 %collective-permute-start.11 = (f32[6,64,256]{2,1,0:T(8,128)S(1)}, f32[6,64,256]{2,1,0:T(8,128)}, u32[]{:S(2)}, u32[]{:S(2)}) collective-permute-start(f32[6,64,256]{2,1,0:T(8,128)S(1)} %bitcast.20), channel_id=1, source_target_pairs={{0,8},{8,0},{16,24},{24,16},{32,40},{40,32},{48,56},{56,48},{64,72... | collective-permute-start | bytes 1179656 | tf_op jit(solution)/shard_map/ppermute | solution.py:431
  39.5 15.2 %collective-permute-start.13 = (bf16[32,16384]{1,0:T(8,128)(2,1)S(1)}, bf16[32,16384]{1,0:T(8,128)(2,1)}, u32[]{:S(2)}, u32[]{:S(2)}) collective-permute-start(bf16[32,16384]{1,0:T(8,128)(2,1)S(1)} %copy-done), channel_id=1, source_target_pairs={{0,8},{8,0},{16,24},{24,16},{32,40},{40,32},{48,56},{56,48},{64,72... | collective-permute-start | bytes 3145736 | tf_op jit(solution)/shard_map/ppermute | solution.py:431
  40.2 14.5 %collective-permute-start.14 = (bf16[32,8192]{1,0:T(8,128)(2,1)S(1)}, bf16[32,8192]{1,0:T(8,128)(2,1)S(1)}, u32[]{:S(2)}, u32[]{:S(2)}) collective-permute-start(bf16[32,8192]{1,0:T(8,128)(2,1)S(1)} %broadcast_select_fusion), channel_id=1, source_target_pairs={{0,8},{8,0},{16,24},{24,16},{32,40},{40,32},{48,56},{56,48},{64,72... | collective-permute-start | bytes 1572872 | tf_op jit(solution)/shard_map/ppermute | solution.py:431
  41.9 4.3 %collective-permute-start.10 = (bf16[4,32,64]{2,1,0:T(8,128)(2,1)S(1)}, bf16[4,32,64]{2,1,0:T(8,128)(2,1)S(1)}, u32[]{:S(2)}, u32[]{:S(2)}) collective-permute-start(bf16[4,32,64]{2,1,0:T(8,128)(2,1)S(1)} %pad_maximum_fusion.4), channel_id=1, source_target_pairs={{0,32},{8,40},{16,48},{24,56},{32,0},{40,8},{48,16},{56,24},{64,96... | collective-permute-start | bytes 49160 | tf_op jit(solution)/shard_map/ppermute | solution.py:477
  42.0 12.7 %collective-permute-start.12 = (f32[6,32,320]{2,1,0:T(8,128)S(1)}, f32[6,32,320]{2,1,0:T(8,128)S(1)}, u32[]{:S(2)}, u32[]{:S(2)}) collective-permute-start(f32[6,32,320]{2,1,0:T(8,128)S(1)} %broadcast_select_fusion.1), channel_id=1, source_target_pairs={{0,8},{8,0},{16,24},{24,16},{32,40},{40,32},{48,56},{56,48},{64,72... | collective-permute-start | bytes 737288 | tf_op jit(solution)/shard_map/ppermute | solution.py:431
  46.2 3.2 %collective-permute-start.17 = (bf16[8,32,64]{2,1,0:T(8,128)(2,1)S(1)}, bf16[8,32,64]{2,1,0:T(8,128)(2,1)S(1)}, u32[]{:S(2)}, u32[]{:S(2)}) collective-permute-start(bf16[8,32,64]{2,1,0:T(8,128)(2,1)S(1)} %pad_maximum_fusion.3), channel_id=1, source_target_pairs={{0,64},{8,72},{16,80},{24,88},{32,96},{40,104},{48,112},{56,120},{... | collective-permute-start | bytes 98312 | tf_op jit(solution)/shard_map/ppermute | solution.py:477
  49.4 64.0 %collective-permute-start.15 = (bf16[32,32,128]{2,1,0:T(8,128)(2,1)S(1)}, bf16[32,32,128]{2,1,0:T(8,128)(2,1)S(1)}, u32[]{:S(2)}, u32[]{:S(2)}) collective-permute-start(bf16[32,32,128]{2,1,0:T(8,128)(2,1)S(1)} %copy-done.5), channel_id=1, source_target_pairs={{0,1},{1,2},{2,3},{3,4},{4,5},{5,6},{6,7},{7,8},{8,9},{9,10},{10,1... | collective-permute-start | bytes 786440 | tf_op jit(solution)/shard_map/ppermute | solution.py:483
  51.9 69.2 %copy-start.1 = (bf16[64,64,64]{2,1,0:T(8,128)(2,1)S(1)}, bf16[64,64,64]{2,1,0:T(8,128)(2,1)}, u32[]{:S(2)}) copy-start(bf16[64,64,64]{2,1,0:T(8,128)(2,1)} %leaf_transfer.3) | copy-start | bytes 1572868
  51.9 69.1 %copy-start.2 = (bf16[8,64,64]{2,1,0:T(8,128)(2,1)S(1)}, bf16[8,64,64]{2,1,0:T(8,128)(2,1)}, u32[]{:S(2)}) copy-start(bf16[8,64,64]{2,1,0:T(8,128)(2,1)} %parent_transfer.3) | copy-start | bytes 196612
  52.0 69.1 %copy-start.3 = (f32[64,3,64]{2,0,1:T(8,128)S(1)}, f32[64,3,64]{2,0,1:T(8,128)}, u32[]{:S(2)}) copy-start(f32[64,3,64]{2,0,1:T(8,128)} %param.17) | copy-start | bytes 147460
  52.0 69.1 %copy-start.6 = (f32[16,3,64]{2,0,1:T(8,128)S(1)}, f32[16,3,64]{2,0,1:T(8,128)}, u32[]{:S(2)}) copy-start(f32[16,3,64]{2,0,1:T(8,128)} %param.20) | copy-start | bytes 36868
  52.0 69.1 %copy-start.7 = (s32[16,8]{0,1:T(8,128)S(1)}, s32[16,8]{0,1:T(8,128)}, u32[]{:S(2)}) copy-start(s32[16,8]{0,1:T(8,128)} %param.21) | copy-start | bytes 1540
  52.0 61.4 %collective-permute-start.16 = (bf16[32,32,128]{2,1,0:T(8,128)(2,1)S(1)}, bf16[32,32,128]{2,1,0:T(8,128)(2,1)S(1)}, u32[]{:S(2)}, u32[]{:S(2)}) collective-permute-start(bf16[32,32,128]{2,1,0:T(8,128)(2,1)S(1)} %copy-done.5), channel_id=1, source_target_pairs={{1,0},{2,1},{3,2},{4,3},{5,4},{6,5},{7,6},{8,7},{9,8},{10,9},{11,1... | collective-permute-start | bytes 786440 | tf_op jit(solution)/shard_map/ppermute | solution.py:484
  113.4 7.6 %collective-permute-start.18 = (bf16[32,32,256]{2,1,0:T(8,128)(2,1)S(1)}, bf16[32,32,256]{2,1,0:T(8,128)(2,1)S(1)}, u32[]{:S(2)}, u32[]{:S(2)}) collective-permute-start(bf16[32,32,256]{2,1,0:T(8,128)(2,1)S(1)} %get-tuple-element.38), channel_id=1, source_target_pairs={{0,8},{8,0},{16,24},{24,16},{32,40},{40,32},{48,56},{56,48},{64,72... | collective-permute-start | bytes 1572872 | tf_op jit(solution)/shard_map/ppermute | solution.py:431
  (7 other events, 157.4 us)

commit v2 on v1

--- a/solution.py
+++ b/solution.py
@@ -12,6 +12,7 @@
 AXES = ("leaf", "sub")
 LANES = 128
 CHUNK = 16
+PARENTS_PER_STEP = 4
 SMEM = pl.BlockSpec(memory_space=pltpu.SMEM)
 VMEM = pl.BlockSpec(memory_space=pltpu.VMEM)
 PARAMS = pltpu.CompilerParams(vmem_limit_bytes=48 * 1024 * 1024)
@@ -31,7 +32,9 @@
 
 
 def lift_kernel(density, bases, leaf_transfer, parent_transfer, coefficients, partial):
-    fan, _, width = bases.shape
+    width = bases.shape[2]
+    parents = parent_transfer.shape[0]
+    fan = bases.shape[0] // parents
 
     @pl.when(pl.program_id(0) == 0)
     def _():
@@ -39,34 +42,38 @@
 
     values = [
         product(density[:, c * width : (c + 1) * width], bases[c], 1, 1).astype(jnp.bfloat16)
-        for c in range(fan)
+        for c in range(bases.shape[0])
     ]
-    lifted = sum(product(value, leaf_transfer[c]) for c, value in enumerate(values))
-    for c in range(0, fan, 2):
+    for c in range(0, bases.shape[0], 2):
         coefficients[c // 2] = jnp.concatenate(values[c : c + 2], axis=1)
-    partial[...] += product(lifted.astype(jnp.bfloat16), parent_transfer[0])
+    terms = []
+    for p in range(parents):
+        lifted = sum(product(values[c], leaf_transfer[c]) for c in range(p * fan, (p + 1) * fan))
+        terms.append(product(lifted.astype(jnp.bfloat16), parent_transfer[p]))
+    partial[...] += sum(terms)
 
 
 def lift(density, bases, leaf_transfer, parent_transfer):
     leaves, rank, width = bases.shape
     sides = density.shape[0]
     parents = parent_transfer.shape[0]
-    fan = leaves // parents
+    held = PARENTS_PER_STEP
+    part = held * (leaves // parents)
     return pl.pallas_call(
         lift_kernel,
-        grid=(parents,),
+        grid=(parents // held,),
         out_shape=(
             jax.ShapeDtypeStruct((leaves // 2, sides, 2 * rank), jnp.bfloat16),
             jax.ShapeDtypeStruct((sides, rank), jnp.float32),
         ),
         in_specs=[
-            pl.BlockSpec((sides, fan * width), lambda p: (0, p)),
-            pl.BlockSpec((fan, rank, width), lambda p: (p, 0, 0)),
-            pl.BlockSpec((fan, rank, rank), lambda p: (p, 0, 0)),
-            pl.BlockSpec((1, rank, rank), lambda p: (p, 0, 0)),
+            pl.BlockSpec((sides, part * width), lambda p: (0, p)),
+            pl.BlockSpec((part, rank, width), lambda p: (p, 0, 0)),
+            pl.BlockSpec((part, rank, rank), lambda p: (p, 0, 0)),
+            pl.BlockSpec((held, rank, rank), lambda p: (p, 0, 0)),
         ],
         out_specs=(
-            pl.BlockSpec((fan // 2, sides, 2 * rank), lambda p: (p, 0, 0)),
+            pl.BlockSpec((part // 2, sides, 2 * rank), lambda p: (p, 0, 0)),
             pl.BlockSpec((sides, rank), lambda p: (0, 0)),
         ),
         compiler_params=pltpu.CompilerParams(vmem_limit_bytes=60 * 1024 * 1024),
@@ -199,7 +206,7 @@
         sums[t] = jnp.zeros(sums.shape[1:], sums.dtype)
         return 0
 
-    lax.fori_loop(0, leaves, prepare, 0, unroll=8)
+    lax.fori_loop(0, leaves, prepare, 0, unroll=16)
     sums[leaves] = jnp.zeros(sums.shape[1:], sums.dtype)
     for ref in (flux_one, flux_two, block_one, block_two):
         ref[...] = jnp.zeros_like(ref)

time: 133 us -> 129 us (0.970)
  the two profiles are of different devices: /device:TPU:71 before, /device:TPU:61 now
where the time goes in v2:
time: 129 us; the launch traced here: 130 us
  Pallas kernels  76.1 us (59%)
  starting transfers between devices  29.5 us (23%)
  waiting for transfers between devices  20 us (16%)
  local copies, waits for them, and re-layouts  2.14 us (2%)
  other arithmetic  2.02 us (2%)
    pallas_call x1, Pallas kernels, near_field(): pl.pallas_call(near_kernel, out_shape=(jax.ShapeDtypeStruct(half, jnp.flo...  57.9 us
    pallas_call x1, Pallas kernels, finish(): pl.pallas_call(final_kernel, out_shape=jax.ShapeDtypeStruct(density.shape...  14.3 us
    ppermute x3, waiting for transfers between devices, per_device(): lax.ppermute(partial, 'sub', [(i, i ^ step) for i in range(count)])  11.1 us
    ppermute x6, starting transfers between devices, swap(): return lax.ppermute(value, 'leaf', [(i, i ^ 1) for i in range(groups)])  8.21 us
    ppermute x4, starting transfers between devices, per_device(): other = lax.ppermute(coupled, 'leaf', [(i, i ^ step) for i in range(count)])  7.74 us
    ppermute x1, starting transfers between devices, per_device(): den_low = lax.ppermute(density[:, (leaves - reach) * width:], AXES, forward)  6.15 us
    ppermute x4, waiting for transfers between devices, per_device(): other = lax.ppermute(coupled, 'leaf', [(i, i ^ step) for i in range(count)])  6.11 us
    pallas_call x1, Pallas kernels, lift(): pl.pallas_call(lift_kernel, grid=(parents // held,), out_shape=(jax.Shape...  3.95 us
  transfers between devices with their start and end apart: 19, of which 9 were waited for; matrix products, arithmetic and copies ran while one was open for 1% of the time, Pallas kernels for 48%

profile of v2, /device:TPU:61, one launch (start us, length us, event | category | flops | bytes accessed | tf_op | source)
XLA Modules:
  0.0 130.0 jit_solution(1614365681256528712)
XLA Ops:
  0.0 1.0 fusion.2
  1.1 1.8 %pad_maximum_fusion = (f32[6,32,320]{2,1,0:T(8,128)}, f32[6,32,320]{2,1,0:T(8,128)}) fusion(f32[6,32,64]{2,1,0:T(8,128)} %bitcast.17, f32[6,32,256]{2,1,0:T(8,128)S(1)} %get-tuple-element.41, f32[6,32,256]{2,1,0:T(8,128)S(1)} %get-tuple-element.42), kind=kLoop, calls=%fused_computation.1 | loop fusion | flops 122880 | bytes 933888 | tf_op jit(solution)/shard_map/concatenate | solution.py:455
  2.8 1.8 %collective-permute-start.1 = (f32[6,32,320]{2,1,0:T(8,128)}, f32[6,32,320]{2,1,0:T(8,128)S(1)}, u32[]{:S(2)}, u32[]{:S(2)}) collective-permute-start(f32[6,32,320]{2,1,0:T(8,128)} %get-tuple-element.44), channel_id=1, source_target_pairs={{0,1},{1,2},{2,3},{3,4},{4,5},{5,6},{6,7},{7,8},{8,9},{9,10},{10,1... | collective-permute-start | bytes 737288 | tf_op jit(solution)/shard_map/ppermute | solution.py:451
  4.6 3.9 %shard_map.109 = (bf16[32,32,128]{2,1,0:T(8,128)(2,1)}, f32[32,64]{1,0:T(8,128)}) custom-call(bf16[32,16384]{1,0:T(8,128)(2,1)} %density.3, bf16[64,64,256]{2,1,0:T(8,128)(2,1)} %bases.3, bf16[64,64,64]{2,1,0:T(8,128)(2,1)} %leaf_transfer.3, bf16[8,64,64]{2,1,0:T(8,128)(2,1)} %parent_transfer.3), custom_call_target="tpu_custom_call" | custom-call | tf_op jit(solution)/shard_map/pallas_call | solution.py:62
  8.7 1.0 fusion.1
  9.8 6.2 %collective-permute-start.8 = (bf16[32,8192]{1,0:T(8,128)(2,1)}, bf16[32,8192]{1,0:T(8,128)(2,1)S(1)}, u32[]{:S(2)}, u32[]{:S(2)}) collective-permute-start(bf16[32,8192]{1,0:T(8,128)(2,1)} %get-tuple-element.40), channel_id=1, source_target_pairs={{0,1},{1,2},{2,3},{3,4},{4,5},{5,6},{6,7},{7,8},{8,9},{9,10},{10,1... | collective-permute-start | bytes 1572872 | tf_op jit(solution)/shard_map/ppermute | solution.py:457
  16.1 1.1 collective-permute-done.3.other_list
  17.3 1.2 collective-permute-start.4
  18.5 7.8 %collective-permute-done.4 = f32[32,64]{1,0:T(8,128)S(1)} collective-permute-done((f32[32,64]{1,0:T(8,128)S(1)}, f32[32,64]{1,0:T(8,128)S(1)}, u32[]{:S(2)}, u32[]{:S(2)}) %collective-permute-start.4) | collective-permute-done | bytes 8224 | tf_op jit(solution)/shard_map/ppermute | solution.py:472
  26.4 0.8 collective-permute-start.5
  27.2 3.3 %collective-permute-done.5 = f32[32,64]{1,0:T(8,128)S(1)} collective-permute-done((f32[32,64]{1,0:T(8,128)S(1)}, f32[32,64]{1,0:T(8,128)S(1)}, u32[]{:S(2)}, u32[]{:S(2)}) %collective-permute-start.5) | collective-permute-done | bytes 8224 | tf_op jit(solution)/shard_map/ppermute | solution.py:472
  30.5 4.0 %collective-permute-start.6 = (bf16[1,32,64]{2,1,0:T(8,128)(2,1)S(1)}, bf16[1,32,64]{2,1,0:T(8,128)(2,1)S(1)}, u32[]{:S(2)}, u32[]{:S(2)}) collective-permute-start(bf16[1,32,64]{2,1,0:T(8,128)(2,1)S(1)} %fusion), channel_id=1, source_target_pairs={{0,8},{8,0},{16,24},{24,16},{32,40},{40,32},{48,56},{56,48},{64,72... | collective-permute-start | bytes 12296 | tf_op jit(solution)/shard_map/ppermute | solution.py:484
  34.4 0.8 collective-permute-done.6
  35.9 2.0 %collective-permute-done.7 = bf16[2,32,64]{2,1,0:T(8,128)(2,1)S(1)} collective-permute-done((bf16[2,32,64]{2,1,0:T(8,128)(2,1)S(1)}, bf16[2,32,64]{2,1,0:T(8,128)(2,1)S(1)}, u32[]{:S(2)}, u32[]{:S(2)}) %collective-permute-start.7) | collective-permute-done | bytes 8224 | tf_op jit(solution)/shard_map/ppermute | solution.py:484
  38.0 1.6 %collective-permute-start.14 = (bf16[32,8192]{1,0:T(8,128)(2,1)S(1)}, bf16[32,8192]{1,0:T(8,128)(2,1)S(1)}, u32[]{:S(2)}, u32[]{:S(2)}) collective-permute-start(bf16[32,8192]{1,0:T(8,128)(2,1)S(1)} %broadcast_select_fusion), channel_id=1, source_target_pairs={{0,8},{8,0},{16,24},{24,16},{32,40},{40,32},{48,56},{56,48},{64,72... | collective-permute-start | bytes 1572872 | tf_op jit(solution)/shard_map/ppermute | solution.py:438
  39.7 2.7 %collective-permute-start.10 = (bf16[4,32,64]{2,1,0:T(8,128)(2,1)S(1)}, bf16[4,32,64]{2,1,0:T(8,128)(2,1)S(1)}, u32[]{:S(2)}, u32[]{:S(2)}) collective-permute-start(bf16[4,32,64]{2,1,0:T(8,128)(2,1)S(1)} %pad_maximum_fusion.4), channel_id=1, source_target_pairs={{0,32},{8,40},{16,48},{24,56},{32,0},{40,8},{48,16},{56,24},{64,96... | collective-permute-start | bytes 49160 | tf_op jit(solution)/shard_map/ppermute | solution.py:484
  42.8 1.1 collective-permute-done.10
  44.0 1.0 collective-permute-start.17
  45.0 2.2 %collective-permute-done.17 = bf16[8,32,64]{2,1,0:T(8,128)(2,1)S(1)} collective-permute-done((bf16[8,32,64]{2,1,0:T(8,128)(2,1)S(1)}, bf16[8,32,64]{2,1,0:T(8,128)(2,1)S(1)}, u32[]{:S(2)}, u32[]{:S(2)}) %collective-permute-start.17) | collective-permute-done | bytes 32800 | tf_op jit(solution)/shard_map/ppermute | solution.py:484
  47.2 3.3 %collective-permute-start.15 = (bf16[32,32,128]{2,1,0:T(8,128)(2,1)S(1)}, bf16[32,32,128]{2,1,0:T(8,128)(2,1)S(1)}, u32[]{:S(2)}, u32[]{:S(2)}) collective-permute-start(bf16[32,32,128]{2,1,0:T(8,128)(2,1)S(1)} %copy-done.5), channel_id=1, source_target_pairs={{0,1},{1,2},{2,3},{3,4},{4,5},{5,6},{6,7},{7,8},{8,9},{9,10},{10,1... | collective-permute-start | bytes 786440 | tf_op jit(solution)/shard_map/ppermute | solution.py:490
  50.7 57.9 %shard_map.110 = (f32[32,32,256]{2,1,0:T(8,128)S(1)}, bf16[32,32,256]{2,1,0:T(8,128)(2,1)S(1)}) custom-call(s32[2]{0:T(128)S(1)} %pad_add_fusion.1.place, s32[10,64]{1,0:T(8,128)S(1)} %pad_add_fusion.near_list, s32[10,64]{1,0:T(8,128)S(1)} %collective-permute-done.3.other_list, f32[6,64,256]{2,1,0:T(8,128)S(1)} %bitcast.21, ...), custom_call_target="tpu_custom_call" | custom-call | flops 49999998976 | bytes 8000000 | tf_op jit(solution)/shard_map/pallas_call | solution.py:269
  108.7 5.5 %collective-permute-start.18 = (bf16[32,32,256]{2,1,0:T(8,128)(2,1)S(1)}, bf16[32,32,256]{2,1,0:T(8,128)(2,1)S(1)}, u32[]{:S(2)}, u32[]{:S(2)}) collective-permute-start(bf16[32,32,256]{2,1,0:T(8,128)(2,1)S(1)} %get-tuple-element.38), channel_id=1, source_target_pairs={{0,8},{8,0},{16,24},{24,16},{32,40},{40,32},{48,56},{56,48},{64,72... | collective-permute-start | bytes 1572872 | tf_op jit(solution)/shard_map/ppermute | solution.py:438
  114.2 1.5 %collective-permute-done.18.near_back = bf16[32,32,256]{2,1,0:T(8,128)(2,1)S(1)} collective-permute-done((bf16[32,32,256]{2,1,0:T(8,128)(2,1)S(1)}, bf16[32,32,256]{2,1,0:T(8,128)(2,1)S(1)}, u32[]{:S(2)}, u32[]{:S(2)}) %collective-permute-start.18) | collective-permute-done | bytes 524320 | tf_op jit(solution)/shard_map/ppermute | solution.py:438
  115.7 14.3 %shard_map.111 = f32[32,16384]{1,0:T(8,128)} custom-call(s32[2]{0:T(128)S(1)} %pad_add_fusion.1.place, s32[16,64]{1,0:T(8,128)S(1)} %add_bitcast_fusion.far_list, s32[8,16]{1,0:T(8,128)S(1)} %bitcast.23, f32[3,16,64]{2,1,0:T(8,128)S(1)} %bitcast.22, bf16[16,32,64]{2,1,0:T(8,128)(2,1)S(1)} %pad_maximum_fusion.2.coupled, bf16[32,32,128]{2,1,0:T(8,128)(2,1)S(1)} %copy-done.5, ...), custom_call_target="tpu_custom_call" | custom-call | tf_op jit(solution)/shard_map/pallas_call | solution.py:405
  (57 shorter events, 1.7 us)
Async XLA Ops:
  2.8 14.4 %collective-permute-start.1 = (f32[6,32,320]{2,1,0:T(8,128)}, f32[6,32,320]{2,1,0:T(8,128)S(1)}, u32[]{:S(2)}, u32[]{:S(2)}) collective-permute-start(f32[6,32,320]{2,1,0:T(8,128)} %get-tuple-element.44), channel_id=1, source_target_pairs={{0,1},{1,2},{2,3},{3,4},{4,5},{5,6},{6,7},{7,8},{8,9},{9,10},{10,1... | collective-permute-start | bytes 737288 | tf_op jit(solution)/shard_map/ppermute | solution.py:451
  4.6 12.7 %collective-permute-start.2 = (f32[6,32,320]{2,1,0:T(8,128)}, f32[6,32,320]{2,1,0:T(8,128)S(1)}, u32[]{:S(2)}, u32[]{:S(2)}) collective-permute-start(f32[6,32,320]{2,1,0:T(8,128)} %get-tuple-element.43), channel_id=1, source_target_pairs={{1,0},{2,1},{3,2},{4,3},{5,4},{6,5},{7,6},{8,7},{9,8},{10,9},{11,1... | collective-permute-start | bytes 737288 | tf_op jit(solution)/shard_map/ppermute | solution.py:454
  8.6 7.3 %collective-permute-start = (f32[32,64]{1,0:T(8,128)}, f32[32,64]{1,0:T(8,128)S(1)}, u32[]{:S(2)}, u32[]{:S(2)}) collective-permute-start(f32[32,64]{1,0:T(8,128)} %get-tuple-element.22), channel_id=1, source_target_pairs={{0,1},{1,0},{2,3},{3,2},{4,5},{5,4},{6,7},{7,6},{8,9},{9,8},{10,11... | collective-permute-start | bytes 24584 | tf_op jit(solution)/shard_map/ppermute | solution.py:472
  9.8 28.2 %collective-permute-start.8 = (bf16[32,8192]{1,0:T(8,128)(2,1)}, bf16[32,8192]{1,0:T(8,128)(2,1)S(1)}, u32[]{:S(2)}, u32[]{:S(2)}) collective-permute-start(bf16[32,8192]{1,0:T(8,128)(2,1)} %get-tuple-element.40), channel_id=1, source_target_pairs={{0,1},{1,2},{2,3},{3,4},{4,5},{5,6},{6,7},{7,8},{8,9},{9,10},{10,1... | collective-permute-start | bytes 1572872 | tf_op jit(solution)/shard_map/ppermute | solution.py:457
  15.9 22.0 %collective-permute-start.9 = (bf16[32,8192]{1,0:T(8,128)(2,1)}, bf16[32,8192]{1,0:T(8,128)(2,1)S(1)}, u32[]{:S(2)}, u32[]{:S(2)}) collective-permute-start(bf16[32,8192]{1,0:T(8,128)(2,1)} %get-tuple-element.39), channel_id=1, source_target_pairs={{1,0},{2,1},{3,2},{4,3},{5,4},{6,5},{7,6},{8,7},{9,8},{10,9},{11,1... | collective-permute-start | bytes 1572872 | tf_op jit(solution)/shard_map/ppermute | solution.py:458
  16.0 1.3 collective-permute-start.3
  17.3 9.1 %collective-permute-start.4 = (f32[32,64]{1,0:T(8,128)S(1)}, f32[32,64]{1,0:T(8,128)S(1)}, u32[]{:S(2)}, u32[]{:S(2)}) collective-permute-start(f32[32,64]{1,0:T(8,128)S(1)} %add.58), channel_id=1, source_target_pairs={{0,2},{1,3},{2,0},{3,1},{4,6},{5,7},{6,4},{7,5},{8,10},{9,11},{10,... | collective-permute-start | bytes 24584 | tf_op jit(solution)/shard_map/ppermute | solution.py:472
  26.4 4.1 %collective-permute-start.5 = (f32[32,64]{1,0:T(8,128)S(1)}, f32[32,64]{1,0:T(8,128)S(1)}, u32[]{:S(2)}, u32[]{:S(2)}) collective-permute-start(f32[32,64]{1,0:T(8,128)S(1)} %add.65), channel_id=1, source_target_pairs={{0,4},{1,5},{2,6},{3,7},{4,0},{5,1},{6,2},{7,3},{8,12},{9,13},{10,... | collective-permute-start | bytes 24584 | tf_op jit(solution)/shard_map/ppermute | solution.py:472
  30.5 4.8 %collective-permute-start.6 = (bf16[1,32,64]{2,1,0:T(8,128)(2,1)S(1)}, bf16[1,32,64]{2,1,0:T(8,128)(2,1)S(1)}, u32[]{:S(2)}, u32[]{:S(2)}) collective-permute-start(bf16[1,32,64]{2,1,0:T(8,128)(2,1)S(1)} %fusion), channel_id=1, source_target_pairs={{0,8},{8,0},{16,24},{24,16},{32,40},{40,32},{48,56},{56,48},{64,72... | collective-permute-start | bytes 12296 | tf_op jit(solution)/shard_map/ppermute | solution.py:484
  35.3 2.6 %collective-permute-start.7 = (bf16[2,32,64]{2,1,0:T(8,128)(2,1)S(1)}, bf16[2,32,64]{2,1,0:T(8,128)(2,1)S(1)}, u32[]{:S(2)}, u32[]{:S(2)}) collective-permute-start(bf16[2,32,64]{2,1,0:T(8,128)(2,1)S(1)} %pad_maximum_fusion.5), channel_id=1, source_target_pairs={{0,16},{8,24},{16,0},{24,8},{32,48},{40,56},{48,32},{56,40},{64,80... | collective-permute-start | bytes 24584 | tf_op jit(solution)/shard_map/ppermute | solution.py:484
  35.3 15.3 %collective-permute-start.11 = (f32[6,64,256]{2,1,0:T(8,128)S(1)}, f32[6,64,256]{2,1,0:T(8,128)}, u32[]{:S(2)}, u32[]{:S(2)}) collective-permute-start(f32[6,64,256]{2,1,0:T(8,128)S(1)} %bitcast.20), channel_id=1, source_target_pairs={{0,8},{8,0},{16,24},{24,16},{32,40},{40,32},{48,56},{56,48},{64,72... | collective-permute-start | bytes 1179656 | tf_op jit(solution)/shard_map/ppermute | solution.py:438
  35.8 14.9 %collective-permute-start.13 = (bf16[32,16384]{1,0:T(8,128)(2,1)S(1)}, bf16[32,16384]{1,0:T(8,128)(2,1)}, u32[]{:S(2)}, u32[]{:S(2)}) collective-permute-start(bf16[32,16384]{1,0:T(8,128)(2,1)S(1)} %copy-done), channel_id=1, source_target_pairs={{0,8},{8,0},{16,24},{24,16},{32,40},{40,32},{48,56},{56,48},{64,72... | collective-permute-start | bytes 3145736 | tf_op jit(solution)/shard_map/ppermute | solution.py:438
  38.0 12.7 %collective-permute-start.14 = (bf16[32,8192]{1,0:T(8,128)(2,1)S(1)}, bf16[32,8192]{1,0:T(8,128)(2,1)S(1)}, u32[]{:S(2)}, u32[]{:S(2)}) collective-permute-start(bf16[32,8192]{1,0:T(8,128)(2,1)S(1)} %broadcast_select_fusion), channel_id=1, source_target_pairs={{0,8},{8,0},{16,24},{24,16},{32,40},{40,32},{48,56},{56,48},{64,72... | collective-permute-start | bytes 1572872 | tf_op jit(solution)/shard_map/ppermute | solution.py:438
  39.7 4.3 %collective-permute-start.10 = (bf16[4,32,64]{2,1,0:T(8,128)(2,1)S(1)}, bf16[4,32,64]{2,1,0:T(8,128)(2,1)S(1)}, u32[]{:S(2)}, u32[]{:S(2)}) collective-permute-start(bf16[4,32,64]{2,1,0:T(8,128)(2,1)S(1)} %pad_maximum_fusion.4), channel_id=1, source_target_pairs={{0,32},{8,40},{16,48},{24,56},{32,0},{40,8},{48,16},{56,24},{64,96... | collective-permute-start | bytes 49160 | tf_op jit(solution)/shard_map/ppermute | solution.py:484
  42.4 8.3 %collective-permute-start.12 = (f32[6,32,320]{2,1,0:T(8,128)S(1)}, f32[6,32,320]{2,1,0:T(8,128)S(1)}, u32[]{:S(2)}, u32[]{:S(2)}) collective-permute-start(f32[6,32,320]{2,1,0:T(8,128)S(1)} %broadcast_select_fusion.1), channel_id=1, source_target_pairs={{0,8},{8,0},{16,24},{24,16},{32,40},{40,32},{48,56},{56,48},{64,72... | collective-permute-start | bytes 737288 | tf_op jit(solution)/shard_map/ppermute | solution.py:438
  44.0 3.2 %collective-permute-start.17 = (bf16[8,32,64]{2,1,0:T(8,128)(2,1)S(1)}, bf16[8,32,64]{2,1,0:T(8,128)(2,1)S(1)}, u32[]{:S(2)}, u32[]{:S(2)}) collective-permute-start(bf16[8,32,64]{2,1,0:T(8,128)(2,1)S(1)} %pad_maximum_fusion.3), channel_id=1, source_target_pairs={{0,64},{8,72},{16,80},{24,88},{32,96},{40,104},{48,112},{56,120},{... | collective-permute-start | bytes 98312 | tf_op jit(solution)/shard_map/ppermute | solution.py:484
  47.2 61.4 %collective-permute-start.15 = (bf16[32,32,128]{2,1,0:T(8,128)(2,1)S(1)}, bf16[32,32,128]{2,1,0:T(8,128)(2,1)S(1)}, u32[]{:S(2)}, u32[]{:S(2)}) collective-permute-start(bf16[32,32,128]{2,1,0:T(8,128)(2,1)S(1)} %copy-done.5), channel_id=1, source_target_pairs={{0,1},{1,2},{2,3},{3,4},{4,5},{5,6},{6,7},{7,8},{8,9},{9,10},{10,1... | collective-permute-start | bytes 786440 | tf_op jit(solution)/shard_map/ppermute | solution.py:490
  50.6 65.2 %copy-start.1 = (bf16[64,64,64]{2,1,0:T(8,128)(2,1)S(1)}, bf16[64,64,64]{2,1,0:T(8,128)(2,1)}, u32[]{:S(2)}) copy-start(bf16[64,64,64]{2,1,0:T(8,128)(2,1)} %leaf_transfer.3) | copy-start | bytes 1572868
  50.6 65.2 %copy-start.2 = (bf16[8,64,64]{2,1,0:T(8,128)(2,1)S(1)}, bf16[8,64,64]{2,1,0:T(8,128)(2,1)}, u32[]{:S(2)}) copy-start(bf16[8,64,64]{2,1,0:T(8,128)(2,1)} %parent_transfer.3) | copy-start | bytes 196612
  50.6 65.1 %copy-start.3 = (f32[64,3,64]{2,0,1:T(8,128)S(1)}, f32[64,3,64]{2,0,1:T(8,128)}, u32[]{:S(2)}) copy-start(f32[64,3,64]{2,0,1:T(8,128)} %param.17) | copy-start | bytes 147460
  50.6 65.1 %copy-start.6 = (f32[16,3,64]{2,0,1:T(8,128)S(1)}, f32[16,3,64]{2,0,1:T(8,128)}, u32[]{:S(2)}) copy-start(f32[16,3,64]{2,0,1:T(8,128)} %param.20) | copy-start | bytes 36868
  50.6 65.1 %copy-start.7 = (s32[16,8]{0,1:T(8,128)S(1)}, s32[16,8]{0,1:T(8,128)}, u32[]{:S(2)}) copy-start(s32[16,8]{0,1:T(8,128)} %param.21) | copy-start | bytes 1540
  50.6 58.0 %collective-permute-start.16 = (bf16[32,32,128]{2,1,0:T(8,128)(2,1)S(1)}, bf16[32,32,128]{2,1,0:T(8,128)(2,1)S(1)}, u32[]{:S(2)}, u32[]{:S(2)}) collective-permute-start(bf16[32,32,128]{2,1,0:T(8,128)(2,1)S(1)} %copy-done.5), channel_id=1, source_target_pairs={{1,0},{2,1},{3,2},{4,3},{5,4},{6,5},{7,6},{8,7},{9,8},{10,9},{11,1... | collective-permute-start | bytes 786440 | tf_op jit(solution)/shard_map/ppermute | solution.py:491
  108.7 7.1 %collective-permute-start.18 = (bf16[32,32,256]{2,1,0:T(8,128)(2,1)S(1)}, bf16[32,32,256]{2,1,0:T(8,128)(2,1)S(1)}, u32[]{:S(2)}, u32[]{:S(2)}) collective-permute-start(bf16[32,32,256]{2,1,0:T(8,128)(2,1)S(1)} %get-tuple-element.38), channel_id=1, source_target_pairs={{0,8},{8,0},{16,24},{24,16},{32,40},{40,32},{48,56},{56,48},{64,72... | collective-permute-start | bytes 1572872 | tf_op jit(solution)/shard_map/ppermute | solution.py:438
  (7 other events, 155.3 us)

commit v3 on v2

--- a/solution.py
+++ b/solution.py
@@ -471,8 +471,10 @@
     while step < count:
         partial = partial + lax.ppermute(partial, "sub", [(i, i ^ step) for i in range(count)])
         if step == 1:
-            partial, geo_low, geo_high, other_list = lax.optimization_barrier(
-                (partial, geo_low, geo_high, other_list)
+            partial, geo_low, geo_high = lax.optimization_barrier((partial, geo_low, geo_high))
+        if step == 2:
+            partial, den_low, den_high, other_list = lax.optimization_barrier(
+                (partial, den_low, den_high, other_list)
             )
         step *= 2
     coupled = partial.astype(jnp.bfloat16)[None]
@@ -483,8 +485,6 @@
             coupled, place = lax.optimization_barrier((coupled, place))
         other = lax.ppermute(coupled, "leaf", [(i, i ^ step) for i in range(count)])
         coupled = jnp.concatenate([coupled, other], axis=0)
-        if step == 2:
-            coupled, den_low, den_high = lax.optimization_barrier((coupled, den_low, den_high))
         step *= 2
 
     coef_low = lax.ppermute(coefficients, AXES, forward)

time: 129 us -> 131 us (1.016)
  the two profiles are of different devices: /device:TPU:61 before, /device:TPU:91 now
where the time goes in v3:
time: 131 us; the launch traced here: 132 us
  Pallas kernels  76.7 us (59%)
  starting transfers between devices  28.9 us (22%)
  waiting for transfers between devices  21.8 us (17%)
  local copies, waits for them, and re-layouts  2.37 us (2%)
  other arithmetic  1.86 us (1%)
    pallas_call x1, Pallas kernels, near_field(): pl.pallas_call(near_kernel, out_shape=(jax.ShapeDtypeStruct(half, jnp.flo...  58.4 us
    pallas_call x1, Pallas kernels, finish(): pl.pallas_call(final_kernel, out_shape=jax.ShapeDtypeStruct(density.shape...  14.3 us
    ppermute x3, waiting for transfers between devices, per_device(): lax.ppermute(partial, 'sub', [(i, i ^ step) for i in range(count)])  10.8 us
    ppermute x6, starting transfers between devices, swap(): return lax.ppermute(value, 'leaf', [(i, i ^ 1) for i in range(groups)])  10.8 us
    ppermute x4, starting transfers between devices, per_device(): other = lax.ppermute(coupled, 'leaf', [(i, i ^ step) for i in range(count)])  6.18 us
    ppermute x4, waiting for transfers between devices, per_device(): other = lax.ppermute(coupled, 'leaf', [(i, i ^ step) for i in range(count)])  5.74 us
    ppermute x1, starting transfers between devices, per_device(): lax.ppermute(jnp.concatenate([geometry[:, leaves - reach:], spread], axis...  5.08 us
    pallas_call x1, Pallas kernels, lift(): pl.pallas_call(lift_kernel, grid=(parents // held,), out_shape=(jax.Shape...  3.96 us
  transfers between devices with their start and end apart: 19, of which 9 were waited for; matrix products, arithmetic and copies ran while one was open for 1% of the time, Pallas kernels for 47%

profile of v3, /device:TPU:91, one launch (start us, length us, event | category | flops | bytes accessed | tf_op | source)
XLA Modules:
  0.0 131.8 jit_solution(2364701218929247364)
XLA Ops:
  0.0 2.3 %fusion.1 = (bf16[32,8192]{1,0:T(8,128)(2,1)}, bf16[32,8192]{1,0:T(8,128)(2,1)}) fusion(bf16[32,16384]{1,0:T(8,128)(2,1)} %density.3), kind=kLoop, calls=%fused_computation.14 | loop fusion | bytes 2097152 | tf_op jit(solution)/shard_map/slice | solution.py:458
  2.3 1.5 %collective-permute-start.4 = (bf16[32,8192]{1,0:T(8,128)(2,1)}, bf16[32,8192]{1,0:T(8,128)(2,1)S(1)}, u32[]{:S(2)}, u32[]{:S(2)}) collective-permute-start(bf16[32,8192]{1,0:T(8,128)(2,1)} %get-tuple-element.40), channel_id=1, source_target_pairs={{0,1},{1,2},{2,3},{3,4},{4,5},{5,6},{6,7},{7,8},{8,9},{9,10},{10,1... | collective-permute-start | bytes 1572872 | tf_op jit(solution)/shard_map/ppermute | solution.py:457
  3.8 0.9 pad_maximum_fusion
  4.7 5.1 %collective-permute-start.1 = (f32[6,32,320]{2,1,0:T(8,128)}, f32[6,32,320]{2,1,0:T(8,128)S(1)}, u32[]{:S(2)}, u32[]{:S(2)}) collective-permute-start(f32[6,32,320]{2,1,0:T(8,128)} %get-tuple-element.44), channel_id=1, source_target_pairs={{0,1},{1,2},{2,3},{3,4},{4,5},{5,6},{6,7},{7,8},{8,9},{9,10},{10,1... | collective-permute-start | bytes 737288 | tf_op jit(solution)/shard_map/ppermute | solution.py:451
  9.8 4.0 %shard_map.109 = (bf16[32,32,128]{2,1,0:T(8,128)(2,1)}, f32[32,64]{1,0:T(8,128)}) custom-call(bf16[32,16384]{1,0:T(8,128)(2,1)} %density.3, bf16[64,64,256]{2,1,0:T(8,128)(2,1)} %bases.3, bf16[64,64,64]{2,1,0:T(8,128)(2,1)} %leaf_transfer.3, bf16[8,64,64]{2,1,0:T(8,128)(2,1)} %parent_transfer.3), custom_call_target="tpu_custom_call" | custom-call | tf_op jit(solution)/shard_map/pallas_call | solution.py:62
  13.9 8.1 %collective-permute-done = f32[32,64]{1,0:T(8,128)S(1)} collective-permute-done((f32[32,64]{1,0:T(8,128)}, f32[32,64]{1,0:T(8,128)S(1)}, u32[]{:S(2)}, u32[]{:S(2)}) %collective-permute-start) | collective-permute-done | bytes 8224 | tf_op jit(solution)/shard_map/ppermute | solution.py:472
  22.0 0.7 add.58
  22.7 3.7 %collective-permute-done.2.geo_high.prox_high = f32[6,32,320]{2,1,0:T(8,128)S(1)} collective-permute-done((f32[6,32,320]{2,1,0:T(8,128)}, f32[6,32,320]{2,1,0:T(8,128)S(1)}, u32[]{:S(2)}, u32[]{:S(2)}) %collective-permute-start.2) | collective-permute-done | bytes 245792 | tf_op jit(solution)/shard_map/ppermute | solution.py:454
  26.4 1.9 %collective-permute-start.6 = (s32[10,64]{1,0:T(8,128)S(1)}, s32[10,64]{1,0:T(8,128)S(1)}, u32[]{:S(2)}, u32[]{:S(2)}) collective-permute-start(s32[10,64]{1,0:T(8,128)S(1)} %pad_add_fusion.near_list), channel_id=1, source_target_pairs={{0,8},{8,0},{16,24},{24,16},{32,40},{40,32},{48,56},{56,48},{64,72... | collective-permute-start | bytes 7688 | tf_op jit(solution)/shard_map/ppermute | solution.py:438
  28.4 2.1 %collective-permute-done.3 = f32[32,64]{1,0:T(8,128)S(1)} collective-permute-done((f32[32,64]{1,0:T(8,128)S(1)}, f32[32,64]{1,0:T(8,128)S(1)}, u32[]{:S(2)}, u32[]{:S(2)}) %collective-permute-start.3) | collective-permute-done | bytes 8224 | tf_op jit(solution)/shard_map/ppermute | solution.py:472
  30.5 3.7 %collective-permute-start.7 = (f32[32,64]{1,0:T(8,128)S(1)}, f32[32,64]{1,0:T(8,128)S(1)}, u32[]{:S(2)}, u32[]{:S(2)}) collective-permute-start(f32[32,64]{1,0:T(8,128)S(1)} %add.59), channel_id=1, source_target_pairs={{0,4},{1,5},{2,6},{3,7},{4,0},{5,1},{6,2},{7,3},{8,12},{9,13},{10,... | collective-permute-start | bytes 24584 | tf_op jit(solution)/shard_map/ppermute | solution.py:472
  35.4 3.5 %collective-permute-start.8 = (bf16[1,32,64]{2,1,0:T(8,128)(2,1)S(1)}, bf16[1,32,64]{2,1,0:T(8,128)(2,1)S(1)}, u32[]{:S(2)}, u32[]{:S(2)}) collective-permute-start(bf16[1,32,64]{2,1,0:T(8,128)(2,1)S(1)} %fusion), channel_id=1, source_target_pairs={{0,8},{8,0},{16,24},{24,16},{32,40},{40,32},{48,56},{56,48},{64,72... | collective-permute-start | bytes 12296 | tf_op jit(solution)/shard_map/ppermute | solution.py:486
  39.0 0.8 collective-permute-done.8
  39.7 1.4 %collective-permute-start.9 = (bf16[2,32,64]{2,1,0:T(8,128)(2,1)S(1)}, bf16[2,32,64]{2,1,0:T(8,128)(2,1)S(1)}, u32[]{:S(2)}, u32[]{:S(2)}) collective-permute-start(bf16[2,32,64]{2,1,0:T(8,128)(2,1)S(1)} %pad_maximum_fusion.5), channel_id=1, source_target_pairs={{0,16},{8,24},{16,0},{24,8},{32,48},{40,56},{48,32},{56,40},{64,80... | collective-permute-start | bytes 24584 | tf_op jit(solution)/shard_map/ppermute | solution.py:486
  41.2 0.8 collective-permute-start.14
  42.5 1.6 %collective-permute-start.12 = (f32[6,32,320]{2,1,0:T(8,128)S(1)}, f32[6,32,320]{2,1,0:T(8,128)S(1)}, u32[]{:S(2)}, u32[]{:S(2)}) collective-permute-start(f32[6,32,320]{2,1,0:T(8,128)S(1)} %broadcast_select_fusion.1), channel_id=1, source_target_pairs={{0,8},{8,0},{16,24},{24,16},{32,40},{40,32},{48,56},{56,48},{64,72... | collective-permute-start | bytes 737288 | tf_op jit(solution)/shard_map/ppermute | solution.py:438
  44.1 2.6 %collective-permute-done.10 = bf16[4,32,64]{2,1,0:T(8,128)(2,1)S(1)} collective-permute-done((bf16[4,32,64]{2,1,0:T(8,128)(2,1)S(1)}, bf16[4,32,64]{2,1,0:T(8,128)(2,1)S(1)}, u32[]{:S(2)}, u32[]{:S(2)}) %collective-permute-start.10) | collective-permute-done | bytes 16416 | tf_op jit(solution)/shard_map/ppermute | solution.py:486
  46.7 1.2 collective-permute-start.17
  48.0 2.0 %collective-permute-done.17 = bf16[8,32,64]{2,1,0:T(8,128)(2,1)S(1)} collective-permute-done((bf16[8,32,64]{2,1,0:T(8,128)(2,1)S(1)}, bf16[8,32,64]{2,1,0:T(8,128)(2,1)S(1)}, u32[]{:S(2)}, u32[]{:S(2)}) %collective-permute-start.17) | collective-permute-done | bytes 32800 | tf_op jit(solution)/shard_map/ppermute | solution.py:486
  50.0 1.5 %collective-permute-start.16 = (bf16[32,32,128]{2,1,0:T(8,128)(2,1)S(1)}, bf16[32,32,128]{2,1,0:T(8,128)(2,1)S(1)}, u32[]{:S(2)}, u32[]{:S(2)}) collective-permute-start(bf16[32,32,128]{2,1,0:T(8,128)(2,1)S(1)} %copy-done.5), channel_id=1, source_target_pairs={{1,0},{2,1},{3,2},{4,3},{5,4},{6,5},{7,6},{8,7},{9,8},{10,9},{11,1... | collective-permute-start | bytes 786440 | tf_op jit(solution)/shard_map/ppermute | solution.py:491
  51.6 58.4 %shard_map.110 = (f32[32,32,256]{2,1,0:T(8,128)S(1)}, bf16[32,32,256]{2,1,0:T(8,128)(2,1)S(1)}) custom-call(s32[2]{0:T(128)S(1)} %pad_add_fusion.1.place, s32[10,64]{1,0:T(8,128)S(1)} %pad_add_fusion.near_list, s32[10,64]{1,0:T(8,128)S(1)} %collective-permute-done.6.other_list, f32[6,64,256]{2,1,0:T(8,128)S(1)} %bitcast.21, ...), custom_call_target="tpu_custom_call" | custom-call | flops 49999998976 | bytes 8000000 | tf_op jit(solution)/shard_map/pallas_call | solution.py:269
  110.0 6.0 %collective-permute-start.18 = (bf16[32,32,256]{2,1,0:T(8,128)(2,1)S(1)}, bf16[32,32,256]{2,1,0:T(8,128)(2,1)S(1)}, u32[]{:S(2)}, u32[]{:S(2)}) collective-permute-start(bf16[32,32,256]{2,1,0:T(8,128)(2,1)S(1)} %get-tuple-element.38), channel_id=1, source_target_pairs={{0,8},{8,0},{16,24},{24,16},{32,40},{40,32},{48,56},{56,48},{64,72... | collective-permute-start | bytes 1572872 | tf_op jit(solution)/shard_map/ppermute | solution.py:438
  116.0 1.5 %collective-permute-done.18.near_back = bf16[32,32,256]{2,1,0:T(8,128)(2,1)S(1)} collective-permute-done((bf16[32,32,256]{2,1,0:T(8,128)(2,1)S(1)}, bf16[32,32,256]{2,1,0:T(8,128)(2,1)S(1)}, u32[]{:S(2)}, u32[]{:S(2)}) %collective-permute-start.18) | collective-permute-done | bytes 524320 | tf_op jit(solution)/shard_map/ppermute | solution.py:438
  117.5 14.3 %shard_map.111 = f32[32,16384]{1,0:T(8,128)} custom-call(s32[2]{0:T(128)S(1)} %pad_add_fusion.1.place, s32[16,64]{1,0:T(8,128)S(1)} %add_bitcast_fusion.far_list, s32[8,16]{1,0:T(8,128)S(1)} %bitcast.23, f32[3,16,64]{2,1,0:T(8,128)S(1)} %bitcast.22, bf16[16,32,64]{2,1,0:T(8,128)(2,1)S(1)} %pad_maximum_fusion.2.coupled, bf16[32,32,128]{2,1,0:T(8,128)(2,1)S(1)} %copy-done.5, ...), custom_call_target="tpu_custom_call" | custom-call | tf_op jit(solution)/shard_map/pallas_call | solution.py:405
  (55 shorter events, 2.1 us)
Async XLA Ops:
  2.3 28.2 %collective-permute-start.4 = (bf16[32,8192]{1,0:T(8,128)(2,1)}, bf16[32,8192]{1,0:T(8,128)(2,1)S(1)}, u32[]{:S(2)}, u32[]{:S(2)}) collective-permute-start(bf16[32,8192]{1,0:T(8,128)(2,1)} %get-tuple-element.40), channel_id=1, source_target_pairs={{0,1},{1,2},{2,3},{3,4},{4,5},{5,6},{6,7},{7,8},{8,9},{9,10},{10,1... | collective-permute-start | bytes 1572872 | tf_op jit(solution)/shard_map/ppermute | solution.py:457
  3.8 26.7 %collective-permute-start.5 = (bf16[32,8192]{1,0:T(8,128)(2,1)}, bf16[32,8192]{1,0:T(8,128)(2,1)S(1)}, u32[]{:S(2)}, u32[]{:S(2)}) collective-permute-start(bf16[32,8192]{1,0:T(8,128)(2,1)} %get-tuple-element.39), channel_id=1, source_target_pairs={{1,0},{2,1},{3,2},{4,3},{5,4},{6,5},{7,6},{8,7},{9,8},{10,9},{11,1... | collective-permute-start | bytes 1572872 | tf_op jit(solution)/shard_map/ppermute | solution.py:458
  4.7 18.0 %collective-permute-start.1 = (f32[6,32,320]{2,1,0:T(8,128)}, f32[6,32,320]{2,1,0:T(8,128)S(1)}, u32[]{:S(2)}, u32[]{:S(2)}) collective-permute-start(f32[6,32,320]{2,1,0:T(8,128)} %get-tuple-element.44), channel_id=1, source_target_pairs={{0,1},{1,2},{2,3},{3,4},{4,5},{5,6},{6,7},{7,8},{8,9},{9,10},{10,1... | collective-permute-start | bytes 737288 | tf_op jit(solution)/shard_map/ppermute | solution.py:451
  9.8 16.6 %collective-permute-start.2 = (f32[6,32,320]{2,1,0:T(8,128)}, f32[6,32,320]{2,1,0:T(8,128)S(1)}, u32[]{:S(2)}, u32[]{:S(2)}) collective-permute-start(f32[6,32,320]{2,1,0:T(8,128)} %get-tuple-element.43), channel_id=1, source_target_pairs={{1,0},{2,1},{3,2},{4,3},{5,4},{6,5},{7,6},{8,7},{9,8},{10,9},{11,1... | collective-permute-start | bytes 737288 | tf_op jit(solution)/shard_map/ppermute | solution.py:454
  13.8 8.2 %collective-permute-start = (f32[32,64]{1,0:T(8,128)}, f32[32,64]{1,0:T(8,128)S(1)}, u32[]{:S(2)}, u32[]{:S(2)}) collective-permute-start(f32[32,64]{1,0:T(8,128)} %get-tuple-element.22), channel_id=1, source_target_pairs={{0,1},{1,0},{2,3},{3,2},{4,5},{5,4},{6,7},{7,6},{8,9},{9,8},{10,11... | collective-permute-start | bytes 24584 | tf_op jit(solution)/shard_map/ppermute | solution.py:472
  26.4 4.1 %collective-permute-start.3 = (f32[32,64]{1,0:T(8,128)S(1)}, f32[32,64]{1,0:T(8,128)S(1)}, u32[]{:S(2)}, u32[]{:S(2)}) collective-permute-start(f32[32,64]{1,0:T(8,128)S(1)} %add.58), channel_id=1, source_target_pairs={{0,2},{1,3},{2,0},{3,1},{4,6},{5,7},{6,4},{7,5},{8,10},{9,11},{10,... | collective-permute-start | bytes 24584 | tf_op jit(solution)/shard_map/ppermute | solution.py:472
  26.4 4.1 %collective-permute-start.6 = (s32[10,64]{1,0:T(8,128)S(1)}, s32[10,64]{1,0:T(8,128)S(1)}, u32[]{:S(2)}, u32[]{:S(2)}) collective-permute-start(s32[10,64]{1,0:T(8,128)S(1)} %pad_add_fusion.near_list), channel_id=1, source_target_pairs={{0,8},{8,0},{16,24},{24,16},{32,40},{40,32},{48,56},{56,48},{64,72... | collective-permute-start | bytes 7688 | tf_op jit(solution)/shard_map/ppermute | solution.py:438
  30.5 4.9 %collective-permute-start.7 = (f32[32,64]{1,0:T(8,128)S(1)}, f32[32,64]{1,0:T(8,128)S(1)}, u32[]{:S(2)}, u32[]{:S(2)}) collective-permute-start(f32[32,64]{1,0:T(8,128)S(1)} %add.59), channel_id=1, source_target_pairs={{0,4},{1,5},{2,6},{3,7},{4,0},{5,1},{6,2},{7,3},{8,12},{9,13},{10,... | collective-permute-start | bytes 24584 | tf_op jit(solution)/shard_map/ppermute | solution.py:472
  34.3 15.8 %collective-permute-start.11 = (f32[6,64,256]{2,1,0:T(8,128)S(1)}, f32[6,64,256]{2,1,0:T(8,128)}, u32[]{:S(2)}, u32[]{:S(2)}) collective-permute-start(f32[6,64,256]{2,1,0:T(8,128)S(1)} %bitcast.20), channel_id=1, source_target_pairs={{0,8},{8,0},{16,24},{24,16},{32,40},{40,32},{48,56},{56,48},{64,72... | collective-permute-start | bytes 1179656 | tf_op jit(solution)/shard_map/ppermute | solution.py:438
  34.3 17.3 %collective-permute-start.13 = (bf16[32,16384]{1,0:T(8,128)(2,1)S(1)}, bf16[32,16384]{1,0:T(8,128)(2,1)}, u32[]{:S(2)}, u32[]{:S(2)}) collective-permute-start(bf16[32,16384]{1,0:T(8,128)(2,1)S(1)} %copy-done), channel_id=1, source_target_pairs={{0,8},{8,0},{16,24},{24,16},{32,40},{40,32},{48,56},{56,48},{64,72... | collective-permute-start | bytes 3145736 | tf_op jit(solution)/shard_map/ppermute | solution.py:438
  35.4 4.3 %collective-permute-start.8 = (bf16[1,32,64]{2,1,0:T(8,128)(2,1)S(1)}, bf16[1,32,64]{2,1,0:T(8,128)(2,1)S(1)}, u32[]{:S(2)}, u32[]{:S(2)}) collective-permute-start(bf16[1,32,64]{2,1,0:T(8,128)(2,1)S(1)} %fusion), channel_id=1, source_target_pairs={{0,8},{8,0},{16,24},{24,16},{32,40},{40,32},{48,56},{56,48},{64,72... | collective-permute-start | bytes 12296 | tf_op jit(solution)/shard_map/ppermute | solution.py:486
  39.7 2.6 %collective-permute-start.9 = (bf16[2,32,64]{2,1,0:T(8,128)(2,1)S(1)}, bf16[2,32,64]{2,1,0:T(8,128)(2,1)S(1)}, u32[]{:S(2)}, u32[]{:S(2)}) collective-permute-start(bf16[2,32,64]{2,1,0:T(8,128)(2,1)S(1)} %pad_maximum_fusion.5), channel_id=1, source_target_pairs={{0,16},{8,24},{16,0},{24,8},{32,48},{40,56},{48,32},{56,40},{64,80... | collective-permute-start | bytes 24584 | tf_op jit(solution)/shard_map/ppermute | solution.py:486
  41.2 10.4 %collective-permute-start.14 = (bf16[32,8192]{1,0:T(8,128)(2,1)S(1)}, bf16[32,8192]{1,0:T(8,128)(2,1)S(1)}, u32[]{:S(2)}, u32[]{:S(2)}) collective-permute-start(bf16[32,8192]{1,0:T(8,128)(2,1)S(1)} %broadcast_select_fusion), channel_id=1, source_target_pairs={{0,8},{8,0},{16,24},{24,16},{32,40},{40,32},{48,56},{56,48},{64,72... | collective-permute-start | bytes 1572872 | tf_op jit(solution)/shard_map/ppermute | solution.py:438
  42.4 4.3 %collective-permute-start.10 = (bf16[4,32,64]{2,1,0:T(8,128)(2,1)S(1)}, bf16[4,32,64]{2,1,0:T(8,128)(2,1)S(1)}, u32[]{:S(2)}, u32[]{:S(2)}) collective-permute-start(bf16[4,32,64]{2,1,0:T(8,128)(2,1)S(1)} %pad_maximum_fusion.4), channel_id=1, source_target_pairs={{0,32},{8,40},{16,48},{24,56},{32,0},{40,8},{48,16},{56,24},{64,96... | collective-permute-start | bytes 49160 | tf_op jit(solution)/shard_map/ppermute | solution.py:486
  42.5 9.1 %collective-permute-start.12 = (f32[6,32,320]{2,1,0:T(8,128)S(1)}, f32[6,32,320]{2,1,0:T(8,128)S(1)}, u32[]{:S(2)}, u32[]{:S(2)}) collective-permute-start(f32[6,32,320]{2,1,0:T(8,128)S(1)} %broadcast_select_fusion.1), channel_id=1, source_target_pairs={{0,8},{8,0},{16,24},{24,16},{32,40},{40,32},{48,56},{56,48},{64,72... | collective-permute-start | bytes 737288 | tf_op jit(solution)/shard_map/ppermute | solution.py:438
  46.7 3.2 %collective-permute-start.17 = (bf16[8,32,64]{2,1,0:T(8,128)(2,1)S(1)}, bf16[8,32,64]{2,1,0:T(8,128)(2,1)S(1)}, u32[]{:S(2)}, u32[]{:S(2)}) collective-permute-start(bf16[8,32,64]{2,1,0:T(8,128)(2,1)S(1)} %pad_maximum_fusion.3), channel_id=1, source_target_pairs={{0,64},{8,72},{16,80},{24,88},{32,96},{40,104},{48,112},{56,120},{... | collective-permute-start | bytes 98312 | tf_op jit(solution)/shard_map/ppermute | solution.py:486
  49.9 60.1 %collective-permute-start.15 = (bf16[32,32,128]{2,1,0:T(8,128)(2,1)S(1)}, bf16[32,32,128]{2,1,0:T(8,128)(2,1)S(1)}, u32[]{:S(2)}, u32[]{:S(2)}) collective-permute-start(bf16[32,32,128]{2,1,0:T(8,128)(2,1)S(1)} %copy-done.5), channel_id=1, source_target_pairs={{0,1},{1,2},{2,3},{3,4},{4,5},{5,6},{6,7},{7,8},{8,9},{9,10},{10,1... | collective-permute-start | bytes 786440 | tf_op jit(solution)/shard_map/ppermute | solution.py:490
  50.0 66.0 %copy-start.9 = (s32[64,16]{0,1:T(8,128)S(1)}, s32[64,16]{0,1:T(8,128)}, u32[]{:S(2)}) copy-start(s32[64,16]{0,1:T(8,128)} %param.15) | copy-start | bytes 12292
  50.0 67.5 %copy-start.1 = (bf16[64,64,64]{2,1,0:T(8,128)(2,1)S(1)}, bf16[64,64,64]{2,1,0:T(8,128)(2,1)}, u32[]{:S(2)}) copy-start(bf16[64,64,64]{2,1,0:T(8,128)(2,1)} %leaf_transfer.3) | copy-start | bytes 1572868
  50.0 67.5 %copy-start.2 = (bf16[8,64,64]{2,1,0:T(8,128)(2,1)S(1)}, bf16[8,64,64]{2,1,0:T(8,128)(2,1)}, u32[]{:S(2)}) copy-start(bf16[8,64,64]{2,1,0:T(8,128)(2,1)} %parent_transfer.3) | copy-start | bytes 196612
  50.0 67.5 %copy-start.6 = (f32[16,3,64]{2,0,1:T(8,128)S(1)}, f32[16,3,64]{2,0,1:T(8,128)}, u32[]{:S(2)}) copy-start(f32[16,3,64]{2,0,1:T(8,128)} %param.20) | copy-start | bytes 36868
  50.0 67.5 %copy-start.7 = (s32[16,8]{0,1:T(8,128)S(1)}, s32[16,8]{0,1:T(8,128)}, u32[]{:S(2)}) copy-start(s32[16,8]{0,1:T(8,128)} %param.21) | copy-start | bytes 1540
  50.0 60.0 %collective-permute-start.16 = (bf16[32,32,128]{2,1,0:T(8,128)(2,1)S(1)}, bf16[32,32,128]{2,1,0:T(8,128)(2,1)S(1)}, u32[]{:S(2)}, u32[]{:S(2)}) collective-permute-start(bf16[32,32,128]{2,1,0:T(8,128)(2,1)S(1)} %copy-done.5), channel_id=1, source_target_pairs={{1,0},{2,1},{3,2},{4,3},{5,4},{6,5},{7,6},{8,7},{9,8},{10,9},{11,1... | collective-permute-start | bytes 786440 | tf_op jit(solution)/shard_map/ppermute | solution.py:491
  110.0 7.5 %collective-permute-start.18 = (bf16[32,32,256]{2,1,0:T(8,128)(2,1)S(1)}, bf16[32,32,256]{2,1,0:T(8,128)(2,1)S(1)}, u32[]{:S(2)}, u32[]{:S(2)}) collective-permute-start(bf16[32,32,256]{2,1,0:T(8,128)(2,1)S(1)} %get-tuple-element.38), channel_id=1, source_target_pairs={{0,8},{8,0},{16,24},{24,16},{32,40},{40,32},{48,56},{56,48},{64,72... | collective-permute-start | bytes 1572872 | tf_op jit(solution)/shard_map/ppermute | solution.py:438
  (6 other events, 89.0 us)
